TPU v7x, 32 devices: a whole 2x2x4 slice. The times are simulated.
32 devices in a mesh: dom: 8 (over z, x), group: 4 (over y, core).
Axes of the slice: x: 2, y: 2, z: 4, core: 2. Of those that a mesh axis runs over, the one named last changes fastest.
Arguments:
- embeddings: float32 [131072, 256], P(('dom', 'group')), may hold values from -0.5 to 0.5
- adagrad_state: float32 [131072], P(('dom', 'group')), may hold values from 0.001 to 0.1
- edge_count: int32 [8], P('dom'), may hold values from 1 to 4096
- lhs_owner: int32 [8, 4, 1024, 1], P('dom', 'group'), may hold values from 0 to 31; in each aligned block of 1024 rows (0 to 1023, 1024 to 2047, ..., all dimensions but the last counted through in order) at most 40 rows name the same one
- lhs_row: int32 [8, 4, 1024], P('dom', 'group'), may hold values from 0 to 4095
- rhs_owner: int32 [8, 4, 1024, 1], P('dom', 'group'), may hold values from 0 to 31; in each aligned block of 1024 rows (0 to 1023, 1024 to 2047, ..., all dimensions but the last counted through in order) at most 40 rows name the same one
- rhs_row: int32 [8, 4, 1024], P('dom', 'group'), may hold values from 0 to 4095
- neg_owner: int32 [8, 4, 1024, 1], P('dom', 'group'), may hold values from 0 to 31; in each aligned block of 1024 rows (0 to 1023, 1024 to 2047, ..., all dimensions but the last counted through in order) at most 40 rows name the same one
- neg_row: int32 [8, 4, 1024], P('dom', 'group'), may hold values from 0 to 4095
Outputs:
- new_embeddings: float32 [131072, 256], P(('dom', 'group'))
- new_state: float32 [131072], P(('dom', 'group'))
Inputs may be any that keep to these rules, and one draw needn't show every extreme that they name: `lhs_owner`: in each group (aligned block of 1024 entries) no device number is named more than 40 times. `rhs_owner`: in each group (aligned block of 1024 entries) no device number is named more than 40 times. `neg_owner`: in each group (aligned block of 1024 entries) no device number is named more than 40 times.
All inputs are finite; a program needn't handle non-finite values.
Results may differ from a plain program's by a relative error of at most 0.00077.
Values may be sent and summed in bfloat16 or wider, within the bound.
No kernel may reach another device: no remote copies, remote signals or barrier semaphores. Data moves between devices by JAX's collectives and lax.ppermute only.
A program may use at most 64 MiB of HBM per device.

v0:
```python
from functools import partial

import jax
import jax.numpy as jnp
from jax import lax
from jax.sharding import PartitionSpec as P

learn_rate = 0.1
adagrad_eps = 1e-06
across_rows = (((0,), (0,)), ((), ()))


def group_gradients(left_rows, right_rows, shared_rows, live_limit):
    left_wide = left_rows.astype(jnp.float32)
    right_wide = right_rows.astype(jnp.float32)
    positive = jnp.sum(left_wide * right_wide, axis=1)
    contract = (((1,), (1,)), ((), ()))
    shared = lax.dot_general(left_rows, shared_rows, contract, preferred_element_type=jnp.float32)
    inchunk = lax.dot_general(left_rows, right_rows, contract, preferred_element_type=jnp.float32)
    places = jnp.arange(left_rows.shape[0], dtype=jnp.int32)
    live_mask = (places < live_limit).astype(jnp.float32)
    allowed = live_mask[None, :] * (places[:, None] != places[None, :]).astype(jnp.float32)
    pos_exp = jnp.exp(positive)
    shared_exp = jnp.exp(shared)
    inchunk_exp = jnp.exp(inchunk) * allowed
    totals = pos_exp + jnp.sum(shared_exp, axis=1) + jnp.sum(inchunk_exp, axis=1)
    weights = live_mask / totals
    pos_grad = live_mask * (pos_exp / totals - 1.0)
    shared_prob = (shared_exp * weights[:, None]).astype(jnp.bfloat16)
    inchunk_prob = (inchunk_exp * weights[:, None]).astype(jnp.bfloat16)
    grad_left = (
        pos_grad[:, None] * right_wide
        + jnp.dot(shared_prob, shared_rows, preferred_element_type=jnp.float32)
        + jnp.dot(inchunk_prob, right_rows, preferred_element_type=jnp.float32)
    )
    grad_right = pos_grad[:, None] * left_wide + lax.dot_general(
        inchunk_prob, left_rows, across_rows, preferred_element_type=jnp.float32
    )
    grad_shared = lax.dot_general(
        shared_prob, left_rows, across_rows, preferred_element_type=jnp.float32
    )
    return (
        grad_left.astype(jnp.bfloat16),
        grad_right.astype(jnp.bfloat16),
        grad_shared.astype(jnp.bfloat16),
    )


def one_hot(spots, width):
    return (spots[:, None] == jnp.arange(width, dtype=jnp.int32)[None, :]).astype(jnp.bfloat16)


def row_spots(owners, is_valid, peer_total, slot_cap):
    count = owners.shape[1]
    order = jnp.arange(count, dtype=jnp.int32)
    lower = (order[:, None] > order[None, :]).astype(jnp.bfloat16)
    matches = (owners[:, :, None] == jnp.arange(peer_total, dtype=jnp.int32)[None, None, :]).astype(
        jnp.bfloat16
    )
    before = jnp.einsum("ij,sjd->sid", lower, matches, preferred_element_type=jnp.float32)
    within = jnp.sum(before * matches.astype(jnp.float32), axis=2).astype(jnp.int32)
    spots = owners * slot_cap + within
    return jnp.where(is_valid[:, None], spots, peer_total * slot_cap)


def kind_bounds(group_len, total_len):
    return [(0, group_len), (group_len, 2 * group_len), (2 * group_len, total_len)]


def fill_requests(spot_row, wanted_row, group_len, peer_total, slot_cap):
    width = peer_total * slot_cap
    pieces = []
    for lower_edge, upper_edge in kind_bounds(group_len, spot_row.shape[0]):
        picker = one_hot(spot_row[lower_edge:upper_edge], width)
        wanted_now = wanted_row[lower_edge:upper_edge]
        halves = jnp.stack([wanted_now // 64, wanted_now % 64], axis=1).astype(jnp.bfloat16)
        gathered = lax.dot_general(picker, halves, across_rows, preferred_element_type=jnp.float32)
        pieces.append(
            (gathered[:, 0] * 64.0 + gathered[:, 1]).astype(jnp.int32).reshape(peer_total, slot_cap)
        )
    return jnp.stack(pieces, axis=1).reshape(-1)


def train_slot(arrived, places_now, limit_now, valid_now, group_len, peer_total, slot_cap):
    features = arrived.shape[1]
    width = peer_total * slot_cap
    stacked_in = arrived.reshape(peer_total, 3, slot_cap, features)
    bounds = kind_bounds(group_len, places_now.shape[0])

    def compute(unused):
        pickers = [
            one_hot(places_now[lower_edge:upper_edge], width) for lower_edge, upper_edge in bounds
        ]
        fetched = [
            jnp.dot(
                pickers[kind],
                stacked_in[:, kind].reshape(width, features),
                preferred_element_type=jnp.float32,
            ).astype(jnp.bfloat16)
            for kind in range(3)
        ]
        grads = group_gradients(fetched[0], fetched[1], fetched[2], limit_now)
        placed = [
            lax.dot_general(
                pickers[kind], grads[kind], across_rows, preferred_element_type=jnp.float32
            )
            .astype(jnp.bfloat16)
            .reshape(peer_total, slot_cap, features)
            for kind in range(3)
        ]
        return jnp.stack(placed, axis=1).reshape(peer_total * 3 * slot_cap, features)

    def keep_zero(unused):
        return jnp.zeros(arrived.shape, jnp.bfloat16)

    return lax.cond(valid_now, compute, keep_zero, 0)


def fetch_rows(row_table, asked):
    rows_dev, features = row_table.shape
    block = min(512, rows_dev)
    span = jnp.arange(block, dtype=jnp.int32)

    def add_block(number, total):
        start = number * block
        table_block = lax.dynamic_slice_in_dim(row_table, start, block, 0)
        picker = (asked[:, None] == start + span[None, :]).astype(jnp.bfloat16)
        return total + jnp.dot(picker, table_block, preferred_element_type=jnp.float32)

    total = lax.fori_loop(
        0, rows_dev // block, add_block, jnp.zeros((asked.shape[0], features), jnp.float32)
    )
    return total.astype(jnp.bfloat16)


def spread_rows(asked, returned, rows_dev):
    block = min(512, rows_dev)
    span = jnp.arange(block, dtype=jnp.int32)
    starts = jnp.arange(rows_dev // block, dtype=jnp.int32) * block

    def one_block(start):
        picker = (asked[:, None] == start + span[None, :]).astype(jnp.bfloat16)
        return lax.dot_general(picker, returned, across_rows, preferred_element_type=jnp.float32)

    return lax.map(one_block, starts).reshape(rows_dev, returned.shape[1])


def body(
    embeddings,
    adagrad_state,
    edge_count,
    lhs_owner,
    lhs_row,
    rhs_owner,
    rhs_row,
    neg_owner,
    neg_row,
):
    rows_dev = embeddings.shape[0]
    features = embeddings.shape[1]
    slot_dev = lhs_row.shape[1]
    group_len = lhs_row.shape[2]
    dom_size = lax.axis_size("dom")
    group_size = lax.axis_size("group")
    peer_total = dom_size * group_size
    slot_cap = 5 * group_len // (4 * peer_total)
    stride = 3 * slot_cap
    group_index = lax.axis_index("group")
    local_slots = jnp.arange(slot_dev, dtype=jnp.int32)
    left_index = lhs_owner[0, :, :, 0] * rows_dev + lhs_row[0]
    right_index = rhs_owner[0, :, :, 0] * rows_dev + rhs_row[0]
    neg_index = neg_owner[0, :, :, 0] * rows_dev + neg_row[0]
    slot_number = group_index * slot_dev + local_slots
    limits = jnp.clip(edge_count[0] - slot_number * group_len, 0, group_len)
    is_valid = limits > 0
    all_index = jnp.concatenate([left_index, right_index, neg_index], axis=1)
    owners = all_index // rows_dev
    wanted = all_index % rows_dev
    places = jnp.concatenate(
        [
            row_spots(owners[:, :group_len], is_valid, peer_total, slot_cap),
            row_spots(owners[:, group_len : 2 * group_len], is_valid, peer_total, slot_cap),
            row_spots(owners[:, 2 * group_len :], is_valid, peer_total, slot_cap),
        ],
        axis=1,
    )
    requests = jax.vmap(
        partial(fill_requests, group_len=group_len, peer_total=peer_total, slot_cap=slot_cap)
    )(places, wanted)
    received = lax.all_to_all(
        requests.reshape(slot_dev, peer_total, stride),
        ("dom", "group"),
        split_axis=1,
        concat_axis=1,
        tiled=True,
    )
    row_table = embeddings.astype(jnp.bfloat16)

    def turn(turn_number, totals):
        asked_rows = lax.dynamic_index_in_dim(received, turn_number, 0, keepdims=False)
        answer = fetch_rows(row_table, asked_rows.reshape(-1)).reshape(peer_total, stride, features)
        arrived = lax.all_to_all(answer, ("dom", "group"), split_axis=0, concat_axis=0, tiled=True)
        arrived = arrived.reshape(peer_total * stride, features)
        places_now = lax.dynamic_index_in_dim(places, turn_number, 0, keepdims=False)
        limit_now = lax.dynamic_index_in_dim(limits, turn_number, 0, keepdims=False)
        valid_now = lax.dynamic_index_in_dim(is_valid, turn_number, 0, keepdims=False)
        outgoing = train_slot(
            arrived, places_now, limit_now, valid_now, group_len, peer_total, slot_cap
        )
        returned = lax.all_to_all(
            outgoing.reshape(peer_total, stride, features),
            ("dom", "group"),
            split_axis=0,
            concat_axis=0,
            tiled=True,
        )
        return totals + spread_rows(
            asked_rows.reshape(-1), returned.reshape(-1, features), rows_dev
        )

    gradients = lax.fori_loop(0, slot_dev, turn, jnp.zeros((rows_dev, features), jnp.float32))
    new_state = adagrad_state + jnp.mean(gradients * gradients, axis=1)
    new_embeddings = embeddings - learn_rate * gradients / (
        jnp.sqrt(new_state)[:, None] + adagrad_eps
    )
    return (new_embeddings, new_state)


def solution(mesh):
    return jax.shard_map(
        body,
        mesh=mesh,
        in_specs=(
            P(("dom", "group"), None),
            P(("dom", "group")),
            P("dom"),
            P("dom", "group", None, None),
            P("dom", "group", None),
            P("dom", "group", None, None),
            P("dom", "group", None),
            P("dom", "group", None, None),
            P("dom", "group", None),
        ),
        out_specs=(P(("dom", "group"), None), P(("dom", "group"))),
        check_vma=False,
    )
```

profile of v0, /device:TPU:0, one launch (start us, length us, event | category | flops | bytes accessed | tf_op | source)
XLA Modules:
  0.0 236.3 jit_solution(1486615639391165659)
XLA Ops:
  0.6 0.7 broadcast_multiply_fusion.3
  4.9 0.7 fusion.75
  6.3 0.7 fusion.76
  7.1 0.7 fusion.77
  8.0 1.1 fusion.67
  9.2 1.1 fusion.66
  10.4 1.1 fusion.68
  11.7 0.7 reshape.948
  12.3 7.3 %all-to-all-start = ((s32[1,32,120]{2,0,1:T(1,128)}), s32[1,32,120]{2,0,1:T(1,128)S(1)}, u32[]{:S(2)}, u32[]{:S(2)}) async-start(s32[1,32,120]{2,0,1:T(1,128)} %bitcast.50), calls=%async_computation | async-start | bytes 32768 | tf_op jit(solution)/shard_map/all_to_all | solution.py:190
  19.7 2.4 %convert_element_type.259 = bf16[4096,256]{1,0:T(8,128)(2,1)S(1)} convert(f32[4096,256]{1,0:T(8,128)} %param.15) | non-fusion elementwise | flops 1048576 | bytes 6291456 | tf_op jit(solution)/shard_map/convert_element_type | solution.py:197
  22.1 4.7 %all-to-all-done = s32[1,32,120]{2,0,1:T(1,128)S(1)} async-done(((s32[1,32,120]{2,0,1:T(1,128)}), s32[1,32,120]{2,0,1:T(1,128)S(1)}, u32[]{:S(2)}, u32[]{:S(2)}) %all-to-all-start) | async-done | bytes 15392 | tf_op jit(solution)/shard_map/all_to_all | solution.py:190
  27.3 37.2 %while.39 = (s32[]{:T(128)}, f32[3840,256]{1,0:T(8,128)}, s32[32,120]{1,0:T(8,128)}, bf16[4096,256]{1,0:T(8,128)(2,1)S(1)}, s32[3840]{0:T(1024)S(1)}, /*index=5*/s32[]{:T(128)}, s32[]{:T(128)}, s32[]{:T(128)}, s32[]{:T(128)}) while((s32[]{:T(128)}, f32[3840,256]{1,0:T(8,128)}, s32[32,120]{1,0:T(8,128)}, ...), condition=%wide.wide.region_4.5_spmd.clone, body=%wide.wide.region_3.4_spmd.clone.sunk | while | flops 1010565632 | bytes 8147101 | solution.py:130
  27.3 3.3 %fusion.145 = f32[3840,256]{1,0:T(8,128)} fusion(f32[3840,256]{1,0:T(8,128)} %get-tuple-element.375, s32[512]{0:T(512)S(1)} %iota_add_fusion.7, s32[3840]{0:T(1024)S(1)} %get-tuple-element.387, pred[]{:T(512)S(6)} %compare.30, bf16[4096,256]{1,0:T(8,128)(2,1)S(1)} %get-tuple-element.386, s32[]{:T(128)S(6)} %select_n.123), kind=kOutput, calls=%fused_computation.57.clone.clone.1 | convolution fusion | flops 1010565120 | bytes 8144901 | tf_op jit(solution)/shard_map/while/body/eval_jaxpr/while/body/eval_jaxpr/dot_general | solution.py:128
  30.6 4.8 %fusion.145 = f32[3840,256]{1,0:T(8,128)} fusion(f32[3840,256]{1,0:T(8,128)} %get-tuple-element.375, s32[512]{0:T(512)S(1)} %iota_add_fusion.7, s32[3840]{0:T(1024)S(1)} %get-tuple-element.387, pred[]{:T(512)S(6)} %compare.30, bf16[4096,256]{1,0:T(8,128)(2,1)S(1)} %get-tuple-element.386, s32[]{:T(128)S(6)} %select_n.123), kind=kOutput, calls=%fused_computation.57.clone.clone.1 | convolution fusion | flops 1010565120 | bytes 8144901 | tf_op jit(solution)/shard_map/while/body/eval_jaxpr/while/body/eval_jaxpr/dot_general | solution.py:128
  35.5 4.8 %fusion.145 = f32[3840,256]{1,0:T(8,128)} fusion(f32[3840,256]{1,0:T(8,128)} %get-tuple-element.375, s32[512]{0:T(512)S(1)} %iota_add_fusion.7, s32[3840]{0:T(1024)S(1)} %get-tuple-element.387, pred[]{:T(512)S(6)} %compare.30, bf16[4096,256]{1,0:T(8,128)(2,1)S(1)} %get-tuple-element.386, s32[]{:T(128)S(6)} %select_n.123), kind=kOutput, calls=%fused_computation.57.clone.clone.1 | convolution fusion | flops 1010565120 | bytes 8144901 | tf_op jit(solution)/shard_map/while/body/eval_jaxpr/while/body/eval_jaxpr/dot_general | solution.py:128
  40.3 4.8 %fusion.145 = f32[3840,256]{1,0:T(8,128)} fusion(f32[3840,256]{1,0:T(8,128)} %get-tuple-element.375, s32[512]{0:T(512)S(1)} %iota_add_fusion.7, s32[3840]{0:T(1024)S(1)} %get-tuple-element.387, pred[]{:T(512)S(6)} %compare.30, bf16[4096,256]{1,0:T(8,128)(2,1)S(1)} %get-tuple-element.386, s32[]{:T(128)S(6)} %select_n.123), kind=kOutput, calls=%fused_computation.57.clone.clone.1 | convolution fusion | flops 1010565120 | bytes 8144901 | tf_op jit(solution)/shard_map/while/body/eval_jaxpr/while/body/eval_jaxpr/dot_general | solution.py:128
  45.2 4.8 %fusion.145 = f32[3840,256]{1,0:T(8,128)} fusion(f32[3840,256]{1,0:T(8,128)} %get-tuple-element.375, s32[512]{0:T(512)S(1)} %iota_add_fusion.7, s32[3840]{0:T(1024)S(1)} %get-tuple-element.387, pred[]{:T(512)S(6)} %compare.30, bf16[4096,256]{1,0:T(8,128)(2,1)S(1)} %get-tuple-element.386, s32[]{:T(128)S(6)} %select_n.123), kind=kOutput, calls=%fused_computation.57.clone.clone.1 | convolution fusion | flops 1010565120 | bytes 8144901 | tf_op jit(solution)/shard_map/while/body/eval_jaxpr/while/body/eval_jaxpr/dot_general | solution.py:128
  50.0 4.8 %fusion.145 = f32[3840,256]{1,0:T(8,128)} fusion(f32[3840,256]{1,0:T(8,128)} %get-tuple-element.375, s32[512]{0:T(512)S(1)} %iota_add_fusion.7, s32[3840]{0:T(1024)S(1)} %get-tuple-element.387, pred[]{:T(512)S(6)} %compare.30, bf16[4096,256]{1,0:T(8,128)(2,1)S(1)} %get-tuple-element.386, s32[]{:T(128)S(6)} %select_n.123), kind=kOutput, calls=%fused_computation.57.clone.clone.1 | convolution fusion | flops 1010565120 | bytes 8144901 | tf_op jit(solution)/shard_map/while/body/eval_jaxpr/while/body/eval_jaxpr/dot_general | solution.py:128
  54.8 4.8 %fusion.145 = f32[3840,256]{1,0:T(8,128)} fusion(f32[3840,256]{1,0:T(8,128)} %get-tuple-element.375, s32[512]{0:T(512)S(1)} %iota_add_fusion.7, s32[3840]{0:T(1024)S(1)} %get-tuple-element.387, pred[]{:T(512)S(6)} %compare.30, bf16[4096,256]{1,0:T(8,128)(2,1)S(1)} %get-tuple-element.386, s32[]{:T(128)S(6)} %select_n.123), kind=kOutput, calls=%fused_computation.57.clone.clone.1 | convolution fusion | flops 1010565120 | bytes 8144901 | tf_op jit(solution)/shard_map/while/body/eval_jaxpr/while/body/eval_jaxpr/dot_general | solution.py:128
  59.7 4.8 %fusion.145 = f32[3840,256]{1,0:T(8,128)} fusion(f32[3840,256]{1,0:T(8,128)} %get-tuple-element.375, s32[512]{0:T(512)S(1)} %iota_add_fusion.7, s32[3840]{0:T(1024)S(1)} %get-tuple-element.387, pred[]{:T(512)S(6)} %compare.30, bf16[4096,256]{1,0:T(8,128)(2,1)S(1)} %get-tuple-element.386, s32[]{:T(128)S(6)} %select_n.123), kind=kOutput, calls=%fused_computation.57.clone.clone.1 | convolution fusion | flops 1010565120 | bytes 8144901 | tf_op jit(solution)/shard_map/while/body/eval_jaxpr/while/body/eval_jaxpr/dot_general | solution.py:128
  64.5 3.6 %convert_element_type.260 = bf16[3840,256]{1,0:T(8,128)(2,1)} convert(f32[3840,256]{1,0:T(8,128)} %get-tuple-element.175) | non-fusion elementwise | flops 983040 | bytes 5898240 | tf_op jit(solution)/shard_map/while/body/eval_jaxpr/convert_element_type | solution.py:133
  68.1 2.7 %all-to-all-start.1 = ((bf16[32,120,256]{2,1,0:T(8,128)(2,1)}), bf16[32,120,256]{2,1,0:T(8,128)(2,1)S(1)}, u32[]{:S(2)}, u32[]{:S(2)}) async-start(bf16[32,120,256]{2,1,0:T(8,128)(2,1)} %bitcast.116), calls=%async_computation.1 | async-start | bytes 3932160 | tf_op jit(solution)/shard_map/while/body/eval_jaxpr/all_to_all | solution.py:202
  70.8 45.9 %all-to-all-done.1 = bf16[32,120,256]{2,1,0:T(8,128)(2,1)S(1)} async-done(((bf16[32,120,256]{2,1,0:T(8,128)(2,1)}), bf16[32,120,256]{2,1,0:T(8,128)(2,1)S(1)}, u32[]{:S(2)}, u32[]{:S(2)}) %all-to-all-start.1) | async-done | bytes 1966112 | tf_op jit(solution)/shard_map/while/body/eval_jaxpr/all_to_all | solution.py:202
  116.7 25.1 %conditional.1 = (bf16[3840,256]{1,0:T(8,128)(2,1)}) conditional(s32[]{:T(128)} %convert_element_type.258, () %tuple.35, (s32[1,3072]{1,0:T(1,128)S(1)}, s32[1]{0:T(128)}, bf16[32,120,256]{2,1,0:T(8,128)(2,1)S(1)}) %tuple.37), branch_computations={%region_5.6_spmd, %region_6.10_spmd} | conditional | flops 7285578752 | bytes 66707500 | solution.py:116
  116.9 1.4 fusion.28
  118.2 1.4 fusion.33
  119.6 2.8 %fusion.10 = (f32[1024]{0:T(1024)S(1)}, f32[1024,1024]{0,1:T(8,128)}) fusion(f32[1024]{0:T(1024)S(1)} %fusion.35, bf16[1024,256]{0,1:T(8,128)(2,1)S(1)} %fusion.28, bf16[1024,256]{0,1:T(8,128)(2,1)S(1)} %get-tuple-element.243), kind=kOutput, calls=%fused_computation.16 | convolution fusion | flops 541064192 | bytes 5251072 | tf_op jit(solution)/shard_map/while/body/eval_jaxpr/cond/branch_1_fun/dot_general | solution.py:19
  122.4 1.1 fusion.30
  123.5 0.7 exponential_reduce_fusion
  124.2 2.0 copy-done
  126.2 0.8 convolution_add_fusion.2
  127.0 4.3 %fusion.24 = bf16[1280,256]{1,0:T(8,128)(2,1)S(1)} fusion(s32[1024]{0:T(1024)S(1)} %bitcast.156, f32[1024,256]{0,1:T(8,128)S(1)} %convolution_add_fusion.2, bf16[1024,256]{0,1:T(8,128)(2,1)S(1)} %get-tuple-element.243, f32[1024,1024]{0,1:T(8,128)} %get-tuple-element.245, f32[1024]{0:T(1024)S(1)} %get-tuple-element.238, f32[1024]{0:T(1024)S(1)} %fusion.35), kind=kOutput, calls=%fused_computation.26 | convolution fusion | flops 1216675840 | bytes 6434816 | tf_op jit(solution)/shard_map/while/body/eval_jaxpr/cond/branch_1_fun/dot_general | solution.py:104
  131.3 4.3 %fusion.21 = bf16[1280,256]{1,0:T(8,128)(2,1)S(1)} fusion(s32[1024]{0:T(1024)S(1)} %bitcast.154, bf16[1024,256]{0,1:T(8,128)(2,1)S(1)} %fusion.28, f32[1024]{0:T(1024)S(1)} %get-tuple-element.237, f32[1024,1024]{0,1:T(8,128)} %get-tuple-element.245, f32[1024]{0:T(1024)S(1)} %get-tuple-element.238, f32[1024]{0:T(1024)S(1)} %fusion.35), kind=kOutput, calls=%fused_computation.25 | convolution fusion | flops 1217200128 | bytes 5390336 | tf_op jit(solution)/shard_map/while/body/eval_jaxpr/cond/branch_1_fun/dot_general | solution.py:104
  135.6 4.6 %fusion.27 = bf16[1280,256]{1,0:T(8,128)(2,1)S(1)} fusion(s32[1024]{0:T(1024)S(1)} %bitcast.152, bf16[1024,256]{0,1:T(8,128)(2,1)S(1)} %fusion.28, f32[1024,1024]{0,1:T(8,128)} %copy-done, f32[1024]{0:T(1024)S(1)} %get-tuple-element.238), kind=kOutput, calls=%fused_computation.27 | convolution fusion | flops 1211957248 | bytes 5382144 | tf_op jit(solution)/shard_map/while/body/eval_jaxpr/cond/branch_1_fun/dot_general | solution.py:104
  140.5 1.4 copy.20
  141.9 2.7 %all-to-all-start.2 = ((bf16[32,120,256]{2,1,0:T(8,128)(2,1)}), bf16[32,120,256]{2,1,0:T(8,128)(2,1)S(1)}, u32[]{:S(2)}, u32[]{:S(2)}) async-start(bf16[32,120,256]{2,1,0:T(8,128)(2,1)} %bitcast.53), calls=%async_computation.2 | async-start | bytes 3932160 | tf_op jit(solution)/shard_map/while/body/eval_jaxpr/all_to_all | solution.py:210
  144.7 45.8 %all-to-all-done.2 = bf16[32,120,256]{2,1,0:T(8,128)(2,1)S(1)} async-done(((bf16[32,120,256]{2,1,0:T(8,128)(2,1)}), bf16[32,120,256]{2,1,0:T(8,128)(2,1)S(1)}, u32[]{:S(2)}, u32[]{:S(2)}) %all-to-all-start.2) | async-done | bytes 1966112 | tf_op jit(solution)/shard_map/while/body/eval_jaxpr/all_to_all | solution.py:210
  190.5 39.5 %while.38 = (s32[]{:T(128)}, f32[8,512,256]{2,1,0:T(8,128)}, s32[32,120]{1,0:T(8,128)}, s32[8]{0:T(128)S(1)}, bf16[3840,256]{1,0:T(8,128)(2,1)S(1)}, /*index=5*/s32[3840]{0:T(1024)S(1)}, s32[]{:T(128)}) while((s32[]{:T(128)}, f32[8,512,256]{2,1,0:T(8,128)}, s32[32,120]{1,0:T(8,128)}, s32[8]{0:T(128)S(1)}, ...), condition=%wide.wide.region_11.12_spmd.clone, body=%wide.wide.region_10.11_spmd.clone.sunk | while | flops 1008599552 | bytes 2510429 | solution.py:145
  191.9 3.6 %fusion.142 = f32[8,512,256]{2,1,0:T(8,128)} fusion(f32[8,512,256]{2,1,0:T(8,128)} %get-tuple-element.400, s32[]{:T(128)} %get-tuple-element.399, bf16[3840,256]{1,0:T(8,128)(2,1)S(1)} %get-tuple-element.410, s32[512]{0:T(512)S(1)} %iota_add_fusion.6, s32[3840]{0:T(1024)S(1)} %get-tuple-element.411), kind=kOutput, calls=%fused_computation.53.clone.clone.1 | convolution fusion | flops 1008599040 | bytes 2508288 | tf_op jit(solution)/shard_map/while/body/eval_jaxpr/while/body/eval_jaxpr/dot_general | solution.py:143
  196.8 3.6 %fusion.142 = f32[8,512,256]{2,1,0:T(8,128)} fusion(f32[8,512,256]{2,1,0:T(8,128)} %get-tuple-element.400, s32[]{:T(128)} %get-tuple-element.399, bf16[3840,256]{1,0:T(8,128)(2,1)S(1)} %get-tuple-element.410, s32[512]{0:T(512)S(1)} %iota_add_fusion.6, s32[3840]{0:T(1024)S(1)} %get-tuple-element.411), kind=kOutput, calls=%fused_computation.53.clone.clone.1 | convolution fusion | flops 1008599040 | bytes 2508288 | tf_op jit(solution)/shard_map/while/body/eval_jaxpr/while/body/eval_jaxpr/dot_general | solution.py:143
  201.8 3.6 %fusion.142 = f32[8,512,256]{2,1,0:T(8,128)} fusion(f32[8,512,256]{2,1,0:T(8,128)} %get-tuple-element.400, s32[]{:T(128)} %get-tuple-element.399, bf16[3840,256]{1,0:T(8,128)(2,1)S(1)} %get-tuple-element.410, s32[512]{0:T(512)S(1)} %iota_add_fusion.6, s32[3840]{0:T(1024)S(1)} %get-tuple-element.411), kind=kOutput, calls=%fused_computation.53.clone.clone.1 | convolution fusion | flops 1008599040 | bytes 2508288 | tf_op jit(solution)/shard_map/while/body/eval_jaxpr/while/body/eval_jaxpr/dot_general | solution.py:143
  206.7 3.6 %fusion.142 = f32[8,512,256]{2,1,0:T(8,128)} fusion(f32[8,512,256]{2,1,0:T(8,128)} %get-tuple-element.400, s32[]{:T(128)} %get-tuple-element.399, bf16[3840,256]{1,0:T(8,128)(2,1)S(1)} %get-tuple-element.410, s32[512]{0:T(512)S(1)} %iota_add_fusion.6, s32[3840]{0:T(1024)S(1)} %get-tuple-element.411), kind=kOutput, calls=%fused_computation.53.clone.clone.1 | convolution fusion | flops 1008599040 | bytes 2508288 | tf_op jit(solution)/shard_map/while/body/eval_jaxpr/while/body/eval_jaxpr/dot_general | solution.py:143
  211.6 3.6 %fusion.142 = f32[8,512,256]{2,1,0:T(8,128)} fusion(f32[8,512,256]{2,1,0:T(8,128)} %get-tuple-element.400, s32[]{:T(128)} %get-tuple-element.399, bf16[3840,256]{1,0:T(8,128)(2,1)S(1)} %get-tuple-element.410, s32[512]{0:T(512)S(1)} %iota_add_fusion.6, s32[3840]{0:T(1024)S(1)} %get-tuple-element.411), kind=kOutput, calls=%fused_computation.53.clone.clone.1 | convolution fusion | flops 1008599040 | bytes 2508288 | tf_op jit(solution)/shard_map/while/body/eval_jaxpr/while/body/eval_jaxpr/dot_general | solution.py:143
  216.6 3.6 %fusion.142 = f32[8,512,256]{2,1,0:T(8,128)} fusion(f32[8,512,256]{2,1,0:T(8,128)} %get-tuple-element.400, s32[]{:T(128)} %get-tuple-element.399, bf16[3840,256]{1,0:T(8,128)(2,1)S(1)} %get-tuple-element.410, s32[512]{0:T(512)S(1)} %iota_add_fusion.6, s32[3840]{0:T(1024)S(1)} %get-tuple-element.411), kind=kOutput, calls=%fused_computation.53.clone.clone.1 | convolution fusion | flops 1008599040 | bytes 2508288 | tf_op jit(solution)/shard_map/while/body/eval_jaxpr/while/body/eval_jaxpr/dot_general | solution.py:143
  221.5 3.6 %fusion.142 = f32[8,512,256]{2,1,0:T(8,128)} fusion(f32[8,512,256]{2,1,0:T(8,128)} %get-tuple-element.400, s32[]{:T(128)} %get-tuple-element.399, bf16[3840,256]{1,0:T(8,128)(2,1)S(1)} %get-tuple-element.410, s32[512]{0:T(512)S(1)} %iota_add_fusion.6, s32[3840]{0:T(1024)S(1)} %get-tuple-element.411), kind=kOutput, calls=%fused_computation.53.clone.clone.1 | convolution fusion | flops 1008599040 | bytes 2508288 | tf_op jit(solution)/shard_map/while/body/eval_jaxpr/while/body/eval_jaxpr/dot_general | solution.py:143
  226.4 3.6 %fusion.142 = f32[8,512,256]{2,1,0:T(8,128)} fusion(f32[8,512,256]{2,1,0:T(8,128)} %get-tuple-element.400, s32[]{:T(128)} %get-tuple-element.399, bf16[3840,256]{1,0:T(8,128)(2,1)S(1)} %get-tuple-element.410, s32[512]{0:T(512)S(1)} %iota_add_fusion.6, s32[3840]{0:T(1024)S(1)} %get-tuple-element.411), kind=kOutput, calls=%fused_computation.53.clone.clone.1 | convolution fusion | flops 1008599040 | bytes 2508288 | tf_op jit(solution)/shard_map/while/body/eval_jaxpr/while/body/eval_jaxpr/dot_general | solution.py:143
  230.0 3.0 %multiply_reduce_fusion = (f32[8,512]{1,0:T(8,128)S(1)}, f32[8,512,256]{2,1,0:T(8,128)S(1)}) fusion(f32[8,512,256]{2,1,0:T(8,128)} %get-tuple-element.176), kind=kLoop, calls=%fused_computation.71 | loop fusion | flops 3141632 | bytes 8404992 | tf_op jit(solution)/shard_map/reduce_sum | solution.py:222
  233.6 2.6 %fusion.59 = f32[4096,256]{1,0:T(8,128)} fusion(f32[4096,256]{1,0:T(8,128)S(1)} %copy-done.1, f32[8,512,256]{2,1,0:T(8,128)S(1)} %get-tuple-element.249, f32[4096]{0:T(1024)S(1)} %get-tuple-element.224), kind=kLoop, calls=%fused_computation.70 | loop fusion | flops 2097152 | bytes 12599296 | tf_op jit(solution)/shard_map/sub | solution.py:223
  (70 shorter events, 16.6 us)
Async XLA Ops:
  12.3 14.4 %all-to-all-start = ((s32[1,32,120]{2,0,1:T(1,128)}), s32[1,32,120]{2,0,1:T(1,128)S(1)}, u32[]{:S(2)}, u32[]{:S(2)}) async-start(s32[1,32,120]{2,0,1:T(1,128)} %bitcast.50), calls=%async_computation | async-start | bytes 32768 | tf_op jit(solution)/shard_map/all_to_all | solution.py:190
  26.7 0.6 copy-start.2
  68.1 48.6 %all-to-all-start.1 = ((bf16[32,120,256]{2,1,0:T(8,128)(2,1)}), bf16[32,120,256]{2,1,0:T(8,128)(2,1)S(1)}, u32[]{:S(2)}, u32[]{:S(2)}) async-start(bf16[32,120,256]{2,1,0:T(8,128)(2,1)} %bitcast.116), calls=%async_computation.1 | async-start | bytes 3932160 | tf_op jit(solution)/shard_map/while/body/eval_jaxpr/all_to_all | solution.py:202
  116.7 27.9 %copy-start.3 = (s32[32,120]{1,0:T(8,128)S(1)}, s32[32,120]{1,0:T(8,128)}, u32[]{:S(2)}) copy-start(s32[32,120]{1,0:T(8,128)} %get-tuple-element.419) | copy-start | bytes 46084
  124.2 2.0 copy-start
  141.9 48.6 %all-to-all-start.2 = ((bf16[32,120,256]{2,1,0:T(8,128)(2,1)}), bf16[32,120,256]{2,1,0:T(8,128)(2,1)S(1)}, u32[]{:S(2)}, u32[]{:S(2)}) async-start(bf16[32,120,256]{2,1,0:T(8,128)(2,1)} %bitcast.53), calls=%async_computation.2 | async-start | bytes 3932160 | tf_op jit(solution)/shard_map/while/body/eval_jaxpr/all_to_all | solution.py:210
  230.0 3.0 %copy-start.4 = (f32[4096]{0:T(1024)S(1)}, f32[4096]{0:T(1024)}, u32[]{:S(2)}) copy-start(f32[4096]{0:T(1024)} %param.16) | copy-start | bytes 49156
  230.0 3.6 %copy-start.1 = (f32[4096,256]{1,0:T(8,128)S(1)}, f32[4096,256]{1,0:T(8,128)}, u32[]{:S(2)}) copy-start(f32[4096,256]{1,0:T(8,128)} %param.15) | copy-start | bytes 12582916
where the time goes:
time: 237 us; the launch traced here: 236 us
  waiting for transfers between devices  96.4 us (41%)
  matrix products  92.5 us (39%)
  other arithmetic  22.5 us (9%)
  starting transfers between devices  12.7 us (5%)
  local copies, waits for them, and re-layouts  10.5 us (4%)
    all_to_all x1, waiting for transfers between devices, turn(): lax.all_to_all(answer, ('dom', 'group'), split_axis=0, concat_axis=0, til...  45.9 us
    all_to_all x1, waiting for transfers between devices, turn(): lax.all_to_all(outgoing.reshape(peer_total, stride, features), ('dom', 'g...  45.8 us
    dot_general x8, matrix products, add_block(): jnp.dot(picker, table_block, preferred_element_type=jnp.float32)  37.1 us
    dot_general x8, matrix products, one_block(): lax.dot_general(picker, returned, across_rows, preferred_element_type=jnp...  28.6 us
    dot_general x3, matrix products, compute(): lax.dot_general(pickers[kind], grads[kind], across_rows, preferred_elemen...  13.2 us
    all_to_all x1, starting transfers between devices, body(): lax.all_to_all(requests.reshape(slot_dev, peer_total, stride), ('dom', 'g...  7.3 us
    add x8, other arithmetic, one_block(): picker = (asked[:, None] == start + span[None, :]).astype(jnp.bfloat16)  5.52 us
    dynamic_slice x8, local copies, waits for them, and re-layouts, spread_rows(): return lax.map(one_block, starts).reshape(rows_dev, returned.shape[1])  5.3 us
  transfers between devices with their start and end apart: 3, of which 3 were waited for; matrix products, arithmetic and copies ran while one was open for 1% of the time, Pallas kernels for 0%

commit v1 on v0

v1 whole, which is shorter than its diff:
```python
from functools import partial

import jax
import jax.numpy as jnp
from jax import lax
from jax.experimental import pallas as pl
from jax.experimental.pallas import tpu as pltpu
from jax.sharding import PartitionSpec as P

learn_rate = 0.1
adagrad_eps = 1e-06
lanes = 128
batch = 4
in_vmem = pl.BlockSpec(memory_space=pltpu.VMEM)
in_smem = pl.BlockSpec(memory_space=pltpu.SMEM)
by_rows = (((1,), (1,)), ((), ()))
f32, bf16, i32 = jnp.float32, jnp.bfloat16, jnp.int32


def params(mib):
    return pltpu.CompilerParams(vmem_limit_bytes=mib * 2**20)


def mul(a, b):
    return jnp.dot(a, b, preferred_element_type=f32)


def mul_t(a, b):
    return lax.dot_general(a, b, by_rows, preferred_element_type=f32)


def iota(shape, dim):
    return lax.broadcasted_iota(i32, shape, dim)


def prep_kernel(rows_dev, limit_ref, *refs):
    index_refs, (ask_ref, spot_ref, fill_ref) = refs[:6], refs[6:]
    peers, stride = ask_ref.shape
    cap = stride // 3
    count = index_refs[0].shape[1]
    part = min(256, count)
    upper = (iota((part, part), 0) < iota((part, part), 1)).astype(f32).astype(bf16)
    peer_of = iota((peers, count), 0)
    slot_of = iota((stride, count), 0)
    spot_ref[...] = jnp.zeros(spot_ref.shape, f32)
    high = low = there = jnp.zeros((peers, stride), f32)
    for kind in range(3):
        owner = index_refs[2 * kind][...]
        row = index_refs[2 * kind + 1][...]
        match = (owner == peer_of).astype(f32)
        seen = jnp.zeros((peers, 1), f32)
        ranks = []
        for start in range(0, count, part):
            now = match[:, start : start + part]
            before = mul(now.astype(bf16), upper) + seen
            seen = seen + jnp.sum(now, axis=1, keepdims=True)
            ranks.append(jnp.sum(now * before, axis=0, keepdims=True))
        rank = jnp.concatenate(ranks, axis=1)
        spot_ref[kind : kind + 1, :] = owner.astype(f32) * cap + rank
        slot = (rank.astype(i32) + kind * cap == slot_of).astype(f32)
        match = match.astype(bf16)
        high += mul_t(match, (slot * (row // 64).astype(f32)).astype(bf16))
        low += mul_t(match, (slot * (row % 64).astype(f32)).astype(bf16))
        there += mul_t(match, slot.astype(bf16))
    asked = (high * 64.0 + low).astype(i32)
    asked = jnp.where(there > 0.5, asked, rows_dev)
    ask_ref[...] = jnp.where(limit_ref[0] > 0, asked, -1)
    place = iota((peers, fill_ref.shape[1]), 1) - iota((peers, fill_ref.shape[1]), 0) * cap
    filled = (place >= 0) & (place.astype(f32) < seen)
    fill_ref[...] = jnp.broadcast_to(
        jnp.sum(filled.astype(f32), axis=0, keepdims=True), fill_ref.shape
    )


def prep(limit, indices, peers, cap, rows_dev):
    count = indices[0].shape[1]
    return pl.pallas_call(
        partial(prep_kernel, rows_dev),
        out_shape=(
            jax.ShapeDtypeStruct((peers, 3 * cap), i32),
            jax.ShapeDtypeStruct((8, count), f32),
            jax.ShapeDtypeStruct((8, peers * cap), f32),
        ),
        in_specs=[in_smem] + [in_vmem] * 6,
        out_specs=(in_vmem,) * 3,
        compiler_params=params(32),
        name="prep",
    )(limit, *indices)


def pack_active(asked_s, asked_v, who, packed):
    peers, stride = asked_v.shape
    packed[...] = jnp.full(packed.shape, -1, i32)

    def step(peer, used):
        active = asked_s[peer, 0] >= 0

        @pl.when(active)
        def take():
            who[used] = peer
            packed[used // batch, pl.ds(used % batch, 1), :stride] = asked_v[pl.ds(peer, 1), :]

        return used + active.astype(i32)

    return lax.fori_loop(0, peers, step, 0)


def fetch_kernel(asked_s, asked_v, table_ref, out_ref, who, packed):
    stride = asked_v.shape[1]
    wide = packed.shape[2]
    rows_dev = table_ref.shape[0]
    used = pack_active(asked_s, asked_v, who, packed)
    row_of = iota((wide, rows_dev), 1)

    def block(number, carry):
        columns = jnp.transpose(packed[number])
        picker = jnp.concatenate(
            [
                (columns[:, j : j + 1] == row_of).astype(f32).astype(bf16)
                for j in range(batch)
            ],
            axis=0,
        )
        rows = mul(picker, table_ref[...])
        for j in range(batch):

            @pl.when(number * batch + j < used)
            def put():
                out_ref[who[number * batch + j]] = rows[j * wide : j * wide + stride].astype(bf16)

        return carry

    lax.fori_loop(0, pl.cdiv(used, batch), block, 0)


def active_scratch(peers, stride):
    wide = pl.cdiv(stride, lanes) * lanes
    return [
        pltpu.SMEM((peers,), i32),
        pltpu.VMEM((pl.cdiv(peers, batch), 8, wide), i32),
    ]


def fetch(asked, table):
    peers, stride = asked.shape
    return pl.pallas_call(
        fetch_kernel,
        out_shape=jax.ShapeDtypeStruct((peers, stride, table.shape[1]), bf16),
        in_specs=[in_smem, in_vmem, in_vmem],
        out_specs=in_vmem,
        scratch_shapes=active_scratch(peers, stride),
        compiler_params=params(40),
        name="fetch",
    )(asked, asked, table)


def train_kernel(
    limit_ref, spot_ref, fill_ref, come_ref, go_ref, wide_ref, place_ref, left_ref, right_ref,
    gl_ref, pg_ref, ps_ref, pr_ref
):
    peers, stride, features = come_ref.shape
    cap = stride // 3
    slots = peers * cap
    count = spot_ref.shape[1]
    part = min(256, count)
    limit = limit_ref[0]

    @pl.when(limit > 0)
    def active():
        def split(peer, carry):
            rows = come_ref[peer].astype(f32)
            for kind in range(3):
                wide_ref[kind, pl.ds(pl.multiple_of(peer * cap, 8), cap), :] = rows[
                    kind * cap : kind * cap + cap
                ]
            return carry

        lax.fori_loop(0, peers, split, 0)
        spot_rows = spot_ref[...]
        spot_columns = jnp.transpose(spot_rows)
        slot_across = iota((part, slots), 1).astype(f32)
        for kind, target in ((0, left_ref), (1, right_ref)):
            held = wide_ref[kind].astype(bf16)
            for start in range(0, count, part):
                column = spot_columns[start : start + part, kind : kind + 1]
                picker = (column == slot_across).astype(f32).astype(bf16)
                target[start : start + part, :] = mul(picker, held).astype(bf16)
        shared_rows = wide_ref[2].astype(bf16)
        fill = fill_ref[0:1, :]
        off_diagonal = (iota((part, part), 0) != iota((part, part), 1)).astype(f32)
        for start in range(0, count, part):
            here = slice(start, start + part)
            left = left_ref[here, :]
            left_wide = left.astype(f32)
            right_wide = right_ref[here, :].astype(f32)
            pos_exp = jnp.exp(jnp.sum(left_wide * right_wide, axis=1, keepdims=True))
            shared_exp = jnp.exp(mul_t(left, shared_rows)) * fill
            total = pos_exp + jnp.sum(shared_exp, axis=1, keepdims=True)
            chunk_exps = []
            for other in range(0, count, part):
                chunk_exp = jnp.exp(mul_t(left, right_ref[other : other + part, :]))
                chunk_exp = chunk_exp * (iota((1, part), 1) + other < limit).astype(f32)
                if other == start:
                    chunk_exp = chunk_exp * off_diagonal
                total = total + jnp.sum(chunk_exp, axis=1, keepdims=True)
                chunk_exps.append(chunk_exp)
            live = (iota((part, 1), 0) + start < limit).astype(f32)
            weight = live / total
            pos_grad = live * (pos_exp / total - 1.0)
            shared_prob = (shared_exp * weight).astype(bf16)
            ps_ref[here, :] = shared_prob
            grad = pos_grad * right_wide + mul(shared_prob, shared_rows)
            for other, chunk_exp in zip(range(0, count, part), chunk_exps):
                chunk_prob = (chunk_exp * weight).astype(bf16)
                pr_ref[here, other : other + part] = chunk_prob
                grad = grad + mul(chunk_prob, right_ref[other : other + part, :])
            gl_ref[here, :] = grad.astype(bf16)
            pg_ref[here, :] = pos_grad * left_wide
        left_turned = jnp.transpose(left_ref[...].astype(f32)).astype(bf16)
        place_ref[2] = jnp.transpose(mul(left_turned, ps_ref[...]))
        grad_right = jnp.transpose(mul(left_turned, pr_ref[...])) + pg_ref[...]
        right_ref[...] = grad_right.astype(bf16)
        slot_down = iota((part, count), 0).astype(f32)
        for kind, source in ((0, gl_ref), (1, right_ref)):
            for start in range(0, slots, part):
                picker = (spot_rows[kind : kind + 1, :] - float(start) == slot_down)
                picker = picker.astype(f32).astype(bf16)
                place_ref[kind, start : start + part, :] = mul(picker, source[...])

        def join(peer, carry):
            go_ref[peer] = jnp.concatenate(
                [
                    place_ref[kind, pl.ds(pl.multiple_of(peer * cap, 8), cap), :]
                    for kind in range(3)
                ],
                axis=0,
            ).astype(bf16)
            return carry

        lax.fori_loop(0, peers, join, 0)


def train(limit, spots, fill, arrived):
    peers, stride, features = arrived.shape
    count = spots.shape[1]
    slots = fill.shape[1]
    return pl.pallas_call(
        train_kernel,
        out_shape=jax.ShapeDtypeStruct(arrived.shape, bf16),
        in_specs=[in_smem, in_vmem, in_vmem, in_vmem],
        out_specs=in_vmem,
        scratch_shapes=[
            pltpu.VMEM((3, slots, features), f32),
            pltpu.VMEM((3, slots, features), f32),
            pltpu.VMEM((count, features), bf16),
            pltpu.VMEM((count, features), bf16),
            pltpu.VMEM((count, features), bf16),
            pltpu.VMEM((count, features), f32),
            pltpu.VMEM((count, slots), bf16),
            pltpu.VMEM((count, count), bf16),
        ],
        compiler_params=params(48),
        name="train",
    )(limit, spots, fill, arrived)


def update_kernel(
    asked_s, asked_v, back_ref, table_ref, state_ref, out_ref, new_state_ref, who, packed, held,
    turned, turned_new
):
    peers, stride = asked_v.shape
    wide = packed.shape[2]
    rows_dev, features = table_ref.shape
    total_blocks = pl.cdiv(peers, batch)
    part = min(512, rows_dev)
    per_part = part // lanes
    used = pack_active(asked_s, asked_v, who, packed)
    blocks = pl.cdiv(used, batch)

    def take(number, carry):
        place = pl.ds(pl.multiple_of(number * wide, wide), wide)

        @pl.when(number < used)
        def full():
            rows = back_ref[who[number]].astype(f32)
            if wide > stride:
                rows = jnp.concatenate([rows, jnp.zeros((wide - stride, features), f32)], axis=0)
            held[place, :] = rows.astype(bf16)

        @pl.when(number >= used)
        def empty():
            held[place, :] = jnp.zeros((wide, features), bf16)

        return carry

    lax.fori_loop(0, total_blocks * batch, take, 0)
    state_turned = jnp.transpose(state_ref[...])
    for number in range(rows_dev // part):
        turned[number, :, :per_part] = state_turned[:, number * per_part : (number + 1) * per_part]

    def finish(number, gradients):
        states = turned[number]
        for j in range(per_part):
            grads = gradients[j * lanes : (j + 1) * lanes]
            state = states[:, j : j + 1] + jnp.mean(grads * grads, axis=1, keepdims=True)
            turned_new[number, :, j : j + 1] = state
            place = pl.ds(pl.multiple_of(number * part + j * lanes, lanes), lanes)
            out_ref[place, :] = table_ref[place, :] - learn_rate * grads / (
                jnp.sqrt(state) + adagrad_eps
            )

    def with_blocks(take_blocks):
        def one_part(number, carry):
            row_of = iota((part, wide), 0) + number * part
            picker = jnp.concatenate(
                [
                    (packed[k // batch, k % batch : k % batch + 1, :] == row_of)
                    .astype(f32)
                    .astype(bf16)
                    for k in range(take_blocks * batch)
                ],
                axis=1,
            )
            finish(number, mul(picker, held[: take_blocks * batch * wide, :]))
            return carry

        lax.fori_loop(0, rows_dev // part, one_part, 0)

    first = max(1, total_blocks // 2)
    for take_blocks in range(first, total_blocks + 1):
        chosen = blocks <= first if take_blocks == first else blocks == take_blocks
        pl.when(chosen)(partial(with_blocks, take_blocks))

    for number in range(rows_dev // part):
        new_state_ref[number * per_part : (number + 1) * per_part, :] = jnp.transpose(
            turned_new[number]
        )[:per_part]


def update(asked, returned, table, state):
    peers, stride = asked.shape
    rows_dev, features = table.shape
    wide = pl.cdiv(stride, lanes) * lanes
    part = min(512, rows_dev)
    kept = pl.cdiv(peers, batch) * batch * wide
    new_table, new_state = pl.pallas_call(
        update_kernel,
        out_shape=(
            jax.ShapeDtypeStruct(table.shape, f32),
            jax.ShapeDtypeStruct((rows_dev // lanes, lanes), f32),
        ),
        in_specs=[in_smem, in_vmem, in_vmem, in_vmem, in_vmem],
        out_specs=(in_vmem, in_vmem),
        scratch_shapes=active_scratch(peers, stride)
        + [
            pltpu.VMEM((kept, features), bf16),
            pltpu.VMEM((rows_dev // part, lanes, lanes), f32),
            pltpu.VMEM((rows_dev // part, lanes, lanes), f32),
        ],
        compiler_params=params(48),
        name="update",
    )(asked, asked, returned, table, state.reshape(rows_dev // lanes, lanes))
    return new_table, new_state.reshape(rows_dev)


def body(
    embeddings,
    adagrad_state,
    edge_count,
    lhs_owner,
    lhs_row,
    rhs_owner,
    rhs_row,
    neg_owner,
    neg_row,
):
    axes = ("dom", "group")
    rows_dev = embeddings.shape[0]
    group_len = lhs_row.shape[2]
    peers = lax.axis_size("dom") * lax.axis_size("group")
    cap = pl.cdiv(5 * group_len // (4 * peers), 8) * 8
    limit = jnp.clip(edge_count - lax.axis_index("group") * group_len, 0, group_len)
    indices = [
        x.reshape(1, group_len)
        for x in (lhs_owner, lhs_row, rhs_owner, rhs_row, neg_owner, neg_row)
    ]
    ask, spots, fill = prep(limit, indices, peers, cap, rows_dev)
    asked = lax.all_to_all(ask, axes, split_axis=0, concat_axis=0, tiled=True)
    answer = fetch(asked, embeddings.astype(bf16))
    arrived = lax.all_to_all(answer, axes, split_axis=0, concat_axis=0, tiled=True)
    grads = train(limit, spots, fill, arrived)
    returned = lax.all_to_all(grads, axes, split_axis=0, concat_axis=0, tiled=True)
    return update(asked, returned, embeddings, adagrad_state)


def solution(mesh):
    return jax.shard_map(
        body,
        mesh=mesh,
        in_specs=(
            P(("dom", "group"), None),
            P(("dom", "group")),
            P("dom"),
            P("dom", "group", None, None),
            P("dom", "group", None),
            P("dom", "group", None, None),
            P("dom", "group", None),
            P("dom", "group", None, None),
            P("dom", "group", None),
        ),
        out_specs=(P(("dom", "group"), None), P(("dom", "group"))),
        check_vma=False,
    )
```

time: 237 us -> 150 us (0.63)
  blocking collectives: 0 us -> 96 us
  matrix products: 92.5 us -> 0 us
  waiting for transfers between devices: 96.4 us -> 4.68 us
  Pallas kernels: 0 us -> 31.1 us
  other arithmetic: 22.5 us -> 2.39 us
  local copies, waits for them, and re-layouts: 10.5 us -> 4.12 us
  starting transfers between devices: 12.7 us -> 7.3 us
    all_to_all x0 -> x2, blocking collectives: none -> 96 us  [the longest x1 48.4 us: body(): lax.all_to_all(grads, axes, split_axis=0, concat_axis=0, tiled=True)]
    dot_general x31 -> x0, matrix products: 92.5 us -> none  [the longest x8 37.1 us: add_block(): jnp.dot(picker, table_block, preferred_element_type=jnp.float32)]
    all_to_all x3 -> x1, waiting for transfers between devices: 96.4 us -> 4.68 us  [body(): asked = lax.all_to_all(ask, axes, split_axis=0, concat_axis=0, tiled=True)]
    pallas_call x0 -> x4, Pallas kernels: none -> 31.1 us  [the longest x1 13.9 us: update(): pl.pallas_call(update_kernel, out_shape=(jax.ShapeDtypeStruct(table.shape...]
    add x20 -> x0, other arithmetic: 8.23 us -> none  [the longest x8 5.52 us: one_block(): picker = (asked[:, None] == start + span[None, :]).astype(jnp.bfloat16)]
    all_to_all x3 -> x1, starting transfers between devices: 12.7 us -> 7.3 us  [body(): asked = lax.all_to_all(ask, axes, split_axis=0, concat_axis=0, tiled=True)]
    dynamic_slice x8 -> x0, local copies, waits for them, and re-layouts: 5.3 us -> none  [spread_rows(): return lax.map(one_block, starts).reshape(rows_dev, returned.shape[1])]
    convert_element_type x9 -> x1, other arithmetic: 6.07 us -> 2.39 us  [body(): answer = fetch(asked, embeddings.astype(bf16))]
  transfers between devices with their start and end apart: 3 -> 1, of which waited for: 3 -> 1; matrix products, arithmetic and copies ran while one was open for 1% -> 2% of each run, Pallas kernels for 0% -> 0%
where the time goes in v1:
time: 150 us; the launch traced here: 147 us
  blocking collectives  96 us (64%)
  Pallas kernels  31.1 us (21%)
  starting transfers between devices  7.3 us (5%)
  waiting for transfers between devices  4.68 us (3%)
  local copies, waits for them, and re-layouts  4.12 us (3%)
  other arithmetic  2.39 us (2%)
    all_to_all x1, blocking collectives, body(): lax.all_to_all(grads, axes, split_axis=0, concat_axis=0, tiled=True)  48.4 us
    all_to_all x1, blocking collectives, body(): lax.all_to_all(answer, axes, split_axis=0, concat_axis=0, tiled=True)  47.6 us
    pallas_call x1, Pallas kernels, update(): pl.pallas_call(update_kernel, out_shape=(jax.ShapeDtypeStruct(table.shape...  13.9 us
    pallas_call x1, Pallas kernels, train(): pl.pallas_call(train_kernel, out_shape=jax.ShapeDtypeStruct(arrived.shape...  8.15 us
    all_to_all x1, starting transfers between devices, body(): asked = lax.all_to_all(ask, axes, split_axis=0, concat_axis=0, tiled=True)  7.3 us
    pallas_call x1, Pallas kernels, fetch(): pl.pallas_call(fetch_kernel, out_shape=jax.ShapeDtypeStruct((peers, strid...  6.98 us
    all_to_all x1, waiting for transfers between devices, body(): asked = lax.all_to_all(ask, axes, split_axis=0, concat_axis=0, tiled=True)  4.68 us
    unnamed x16, local copies, waits for them, and re-layouts  4.12 us
  transfers between devices with their start and end apart: 1, of which 1 were waited for; matrix products, arithmetic and copies ran while one was open for 2% of the time, Pallas kernels for 0%

profile of v1, /device:TPU:0, one launch (start us, length us, event | category | flops | bytes accessed | tf_op | source)
XLA Modules:
  0.0 147.0 jit_solution(16668383564503776543)
XLA Ops:
  1.3 0.0 copy-start.2
  1.3 0.7 copy-done.2
  2.0 0.0 copy-start.3
  2.0 0.7 copy-done.3
  2.7 0.0 copy-start.4
  2.7 0.7 copy-done.4
  3.3 0.0 copy-start.5
  3.4 0.7 copy-done.5
  4.0 0.0 copy-start.6
  4.0 0.7 copy-done.6
  4.7 0.0 copy-start.7
  4.7 0.7 copy-done.7
  5.4 2.1 %prep.1 = (s32[32,120]{1,0:T(8,128)}, f32[8,1024]{1,0:T(8,128)S(1)}, f32[8,1280]{1,0:T(8,128)S(1)}) custom-call(s32[1]{0:T(128)S(6)} %min.6.limit_ref, s32[1,1024]{1,0:T(1,128)S(1)} %bitcast.18, s32[1,1024]{1,0:T(1,128)S(1)} %bitcast.19, s32[1,1024]{1,0:T(1,128)S(1)} %bitcast.20, s32[1,1024]{1,0:T(1,128)S(1)} %bitcast.21, s32[1,1024]{1,0:T(1,128)S(1)} %bitcast.22, ...), custom_call_target="tpu_custom_call" | custom-call | tf_op jit(solution)/shard_map/prep/pallas_call | solution.py:77
  7.5 7.3 %all-to-all-start = ((s32[32,1,120]{2,1,0:T(1,128)}), s32[32,1,120]{2,1,0:T(1,128)S(1)}, u32[]{:S(2)}, u32[]{:S(2)}) async-start(s32[32,1,120]{2,1,0:T(1,128)} %bitcast.8), calls=%async_computation | async-start | bytes 32768 | tf_op jit(solution)/shard_map/all_to_all | solution.py:388
  14.8 2.4 %convert_element_type.3.table_ref = bf16[4096,256]{1,0:T(8,128)(2,1)S(1)} convert(f32[4096,256]{1,0:T(8,128)} %table_ref.1) | non-fusion elementwise | flops 1048576 | bytes 6291456 | tf_op jit(solution)/shard_map/convert_element_type | solution.py:389
  17.2 4.7 %all-to-all-done = s32[32,1,120]{2,1,0:T(1,128)S(1)} async-done(((s32[32,1,120]{2,1,0:T(1,128)}), s32[32,1,120]{2,1,0:T(1,128)S(1)}, u32[]{:S(2)}, u32[]{:S(2)}) %all-to-all-start) | async-done | bytes 15392 | tf_op jit(solution)/shard_map/all_to_all | solution.py:388
  21.9 7.0 %fetch.1 = bf16[32,120,256]{2,1,0:T(8,128)(2,1)S(1)} custom-call(s32[32,120]{1,0:T(8,128)S(1)} %bitcast.13, s32[32,120]{1,0:T(8,128)S(1)} %bitcast.14, bf16[4096,256]{1,0:T(8,128)(2,1)S(1)} %convert_element_type.3.table_ref), custom_call_target="tpu_custom_call" | custom-call | tf_op jit(solution)/shard_map/fetch/pallas_call | solution.py:146
  28.9 47.6 %all_to_all.21.come_ref = bf16[32,120,256]{2,1,0:T(8,128)(2,1)S(1)} all-to-all(bf16[32,120,256]{2,1,0:T(8,128)(2,1)S(1)} %fetch.1), channel_id=1, replica_groups=mesh['dom'=8,'group'=4] {'dom','group'}, dimensions={0} | all-to-all | bytes 3932160 | tf_op jit(solution)/shard_map/all_to_all | solution.py:390
  76.5 0.0 copy-start
  76.5 8.1 %train.1 = bf16[32,120,256]{2,1,0:T(8,128)(2,1)S(1)} custom-call(s32[1]{0:T(128)S(6)} %min.6.limit_ref, f32[8,1024]{1,0:T(8,128)S(1)} %get-tuple-element.8.spot_ref, f32[8,1280]{1,0:T(8,128)S(1)} %get-tuple-element.9.fill_ref, bf16[32,120,256]{2,1,0:T(8,128)(2,1)S(1)} %all_to_all.21.come_ref), custom_call_target="tpu_custom_call" | custom-call | tf_op jit(solution)/shard_map/train/pallas_call | solution.py:247
  84.6 0.0 copy-start.1
  84.7 48.4 %all_to_all.22.back_ref = bf16[32,120,256]{2,1,0:T(8,128)(2,1)S(1)} all-to-all(bf16[32,120,256]{2,1,0:T(8,128)(2,1)S(1)} %train.1), channel_id=1, replica_groups=mesh['dom'=8,'group'=4] {'dom','group'}, dimensions={0} | all-to-all | bytes 3932160 | tf_op jit(solution)/shard_map/all_to_all | solution.py:392
  133.1 0.0 copy-done
  133.1 0.0 copy-done.1
  133.1 13.9 %update.1 = (f32[4096,256]{1,0:T(8,128)}, f32[32,128]{1,0:T(8,128)}) custom-call(s32[32,120]{1,0:T(8,128)S(1)} %bitcast.15, s32[32,120]{1,0:T(8,128)S(1)} %bitcast.16, bf16[32,120,256]{2,1,0:T(8,128)(2,1)S(1)} %all_to_all.22.back_ref, f32[4096,256]{1,0:T(8,128)S(1)} %copy-done, f32[32,128]{1,0:T(8,128)S(1)} %bitcast.17), custom_call_target="tpu_custom_call" | custom-call | tf_op jit(solution)/shard_map/update/pallas_call | solution.py:346
Async XLA Ops:
  1.3 0.7 copy-start.2
  2.0 0.7 copy-start.3
  2.7 0.7 copy-start.4
  3.3 0.7 copy-start.5
  4.0 0.7 copy-start.6
  4.7 0.7 copy-start.7
  7.5 14.4 %all-to-all-start = ((s32[32,1,120]{2,1,0:T(1,128)}), s32[32,1,120]{2,1,0:T(1,128)S(1)}, u32[]{:S(2)}, u32[]{:S(2)}) async-start(s32[32,1,120]{2,1,0:T(1,128)} %bitcast.8), calls=%async_computation | async-start | bytes 32768 | tf_op jit(solution)/shard_map/all_to_all | solution.py:388
  76.5 56.6 %copy-start = (f32[4096,256]{1,0:T(8,128)S(1)}, f32[4096,256]{1,0:T(8,128)}, u32[]{:S(2)}) copy-start(f32[4096,256]{1,0:T(8,128)} %table_ref.1) | copy-start | bytes 12582916
  84.6 48.4 %copy-start.1 = (f32[4096]{0:T(1024)S(1)}, f32[4096]{0:T(1024)}, u32[]{:S(2)}) copy-start(f32[4096]{0:T(1024)} %param.10) | copy-start | bytes 49156

commit v2 on v1

--- a/solution.py
+++ b/solution.py
@@ -33,8 +33,19 @@
     return lax.broadcasted_iota(i32, shape, dim)
 
 
-def prep_kernel(rows_dev, limit_ref, *refs):
-    index_refs, (ask_ref, spot_ref, fill_ref) = refs[:6], refs[6:]
+def prep_kernel(
+    rows_dev, count_hbm, *refs
+):
+    index_hbm, (ask_ref, spot_ref, fill_ref, limit_ref) = refs[:6], refs[6:10]
+    index_refs, edges, arrivals = refs[10:16], refs[16], refs[17]
+    copies = [
+        pltpu.make_async_copy(source, target, arrivals.at[number])
+        for number, (source, target) in enumerate(
+            zip((count_hbm, *index_hbm), (edges, *index_refs))
+        )
+    ]
+    for copy in copies:
+        copy.start()
     peers, stride = ask_ref.shape
     cap = stride // 3
     count = index_refs[0].shape[1]
@@ -44,6 +55,10 @@
     slot_of = iota((stride, count), 0)
     spot_ref[...] = jnp.zeros(spot_ref.shape, f32)
     high = low = there = jnp.zeros((peers, stride), f32)
+    for copy in copies:
+        copy.wait()
+    limit = jnp.clip(edges[0] - lax.axis_index("group") * count, 0, count)
+    limit_ref[0] = limit
     for kind in range(3):
         owner = index_refs[2 * kind][...]
         row = index_refs[2 * kind + 1][...]
@@ -64,7 +79,7 @@
         there += mul_t(match, slot.astype(bf16))
     asked = (high * 64.0 + low).astype(i32)
     asked = jnp.where(there > 0.5, asked, rows_dev)
-    ask_ref[...] = jnp.where(limit_ref[0] > 0, asked, -1)
+    ask_ref[...] = jnp.where(limit > 0, asked, -1)
     place = iota((peers, fill_ref.shape[1]), 1) - iota((peers, fill_ref.shape[1]), 0) * cap
     filled = (place >= 0) & (place.astype(f32) < seen)
     fill_ref[...] = jnp.broadcast_to(
@@ -72,73 +87,67 @@
     )
 
 
-def prep(limit, indices, peers, cap, rows_dev):
+def prep(edge_count, indices, peers, cap, rows_dev):
     count = indices[0].shape[1]
+    anywhere = pl.BlockSpec(memory_space=pl.ANY)
     return pl.pallas_call(
         partial(prep_kernel, rows_dev),
         out_shape=(
             jax.ShapeDtypeStruct((peers, 3 * cap), i32),
             jax.ShapeDtypeStruct((8, count), f32),
             jax.ShapeDtypeStruct((8, peers * cap), f32),
+            jax.ShapeDtypeStruct((1,), i32),
         ),
-        in_specs=[in_smem] + [in_vmem] * 6,
-        out_specs=(in_vmem,) * 3,
+        in_specs=[anywhere] * 7,
+        out_specs=(in_vmem, in_vmem, in_vmem, in_smem),
+        scratch_shapes=[pltpu.VMEM((1, count), i32)] * 6
+        + [pltpu.SMEM((1,), i32), pltpu.SemaphoreType.DMA((7,))],
         compiler_params=params(32),
         name="prep",
-    )(limit, *indices)
+    )(edge_count, *indices)
 
 
 def pack_active(asked_s, asked_v, who, packed):
     peers, stride = asked_v.shape
     packed[...] = jnp.full(packed.shape, -1, i32)
-
-    def step(peer, used):
-        active = asked_s[peer, 0] >= 0
-
-        @pl.when(active)
-        def take():
-            who[used] = peer
-            packed[used // batch, pl.ds(used % batch, 1), :stride] = asked_v[pl.ds(peer, 1), :]
-
-        return used + active.astype(i32)
-
-    return lax.fori_loop(0, peers, step, 0)
+    used = 0
+    for peer in range(peers):
+        who[used] = peer
+        packed[pl.ds(used, 1), :stride] = asked_v[peer : peer + 1, :]
+        used = used + (asked_s[peer, 0] >= 0).astype(i32)
+    packed[pl.ds(used, 1), :] = jnp.full((1, packed.shape[1]), -1, i32)
+    return used
 
 
 def fetch_kernel(asked_s, asked_v, table_ref, out_ref, who, packed):
     stride = asked_v.shape[1]
-    wide = packed.shape[2]
+    wide = packed.shape[1]
     rows_dev = table_ref.shape[0]
     used = pack_active(asked_s, asked_v, who, packed)
     row_of = iota((wide, rows_dev), 1)
 
-    def block(number, carry):
-        columns = jnp.transpose(packed[number])
+    def block(first, size):
+        columns = jnp.transpose(packed[pl.ds(pl.multiple_of(first, 8), 8), :])
         picker = jnp.concatenate(
-            [
-                (columns[:, j : j + 1] == row_of).astype(f32).astype(bf16)
-                for j in range(batch)
-            ],
+            [(columns[:, j : j + 1] == row_of).astype(f32).astype(bf16) for j in range(size)],
             axis=0,
         )
         rows = mul(picker, table_ref[...])
-        for j in range(batch):
-
-            @pl.when(number * batch + j < used)
+        for j in range(size):
+
+            @pl.when(first + j < used)
             def put():
-                out_ref[who[number * batch + j]] = rows[j * wide : j * wide + stride].astype(bf16)
-
-        return carry
-
-    lax.fori_loop(0, pl.cdiv(used, batch), block, 0)
+                out_ref[who[first + j]] = rows[j * wide : j * wide + stride].astype(bf16)
+
+    rest = used % 8
+    large = used // 8 + (rest > 4).astype(i32)
+    lax.fori_loop(0, large, lambda number, carry: (block(number * 8, 8), carry)[1], 0)
+    pl.when((rest > 0) & (rest <= 4))(lambda: block(large * 8, 4))
 
 
 def active_scratch(peers, stride):
     wide = pl.cdiv(stride, lanes) * lanes
-    return [
-        pltpu.SMEM((peers,), i32),
-        pltpu.VMEM((pl.cdiv(peers, batch), 8, wide), i32),
-    ]
+    return [pltpu.SMEM((peers + 8,), i32), pltpu.VMEM((pl.cdiv(peers, 8) * 8 + 8, wide), i32)]
 
 
 def fetch(asked, table):
@@ -265,76 +274,86 @@
 
 
 def update_kernel(
-    asked_s, asked_v, back_ref, table_ref, state_ref, out_ref, new_state_ref, who, packed, held,
-    turned, turned_new
+    asked_s, asked_v, back_ref, table_ref, state_ref, out_hbm, new_state_ref, who, packed, held,
+    turned, turned_new, grads_ref, out_ref, left
 ):
     peers, stride = asked_v.shape
-    wide = packed.shape[2]
+    wide = packed.shape[1]
     rows_dev, features = table_ref.shape
     total_blocks = pl.cdiv(peers, batch)
     part = min(512, rows_dev)
+    parts = rows_dev // part
     per_part = part // lanes
     used = pack_active(asked_s, asked_v, who, packed)
     blocks = pl.cdiv(used, batch)
+    if wide > stride:
+        tail = stride // 16 * 16
+        held[:, tail:, :] = jnp.zeros((held.shape[0], wide - tail, features), bf16)
 
     def take(number, carry):
-        place = pl.ds(pl.multiple_of(number * wide, wide), wide)
-
-        @pl.when(number < used)
-        def full():
-            rows = back_ref[who[number]].astype(f32)
-            if wide > stride:
-                rows = jnp.concatenate([rows, jnp.zeros((wide - stride, features), f32)], axis=0)
-            held[place, :] = rows.astype(bf16)
-
-        @pl.when(number >= used)
-        def empty():
-            held[place, :] = jnp.zeros((wide, features), bf16)
-
+        held[number, :stride, :] = back_ref[who[number]]
         return carry
 
-    lax.fori_loop(0, total_blocks * batch, take, 0)
+    def clear(number, carry):
+        held[number] = jnp.zeros((wide, features), bf16)
+        return carry
+
+    lax.fori_loop(0, used, take, 0)
+    lax.fori_loop(used, blocks * batch, clear, 0)
     state_turned = jnp.transpose(state_ref[...])
-    for number in range(rows_dev // part):
+    for number in range(parts):
         turned[number, :, :per_part] = state_turned[:, number * per_part : (number + 1) * per_part]
 
-    def finish(number, gradients):
-        states = turned[number]
+    def leave(number):
+        rows = pl.ds(pl.multiple_of(number * part, part), part)
+        return pltpu.make_async_copy(out_ref.at[rows], out_hbm.at[rows], left.at[number])
+
+    def finish(number):
+        grads = [grads_ref[j * lanes : (j + 1) * lanes, :] for j in range(per_part)]
+        sums = [jnp.sum(g * g, axis=1, keepdims=True) for g in grads]
+        state = turned[number, :, :per_part] + jnp.concatenate(sums, axis=1) * (1.0 / features)
+        turned_new[number, :, :per_part] = state
+        scale = learn_rate / (jnp.sqrt(state) + adagrad_eps)
         for j in range(per_part):
-            grads = gradients[j * lanes : (j + 1) * lanes]
-            state = states[:, j : j + 1] + jnp.mean(grads * grads, axis=1, keepdims=True)
-            turned_new[number, :, j : j + 1] = state
             place = pl.ds(pl.multiple_of(number * part + j * lanes, lanes), lanes)
-            out_ref[place, :] = table_ref[place, :] - learn_rate * grads / (
-                jnp.sqrt(state) + adagrad_eps
-            )
+            out_ref[place, :] = table_ref[place, :] - grads[j] * scale[:, j : j + 1]
 
     def with_blocks(take_blocks):
-        def one_part(number, carry):
+        rows_held = held[: take_blocks * batch].reshape(take_blocks * batch * wide, features)
+
+        def gather(number):
             row_of = iota((part, wide), 0) + number * part
             picker = jnp.concatenate(
                 [
-                    (packed[k // batch, k % batch : k % batch + 1, :] == row_of)
-                    .astype(f32)
-                    .astype(bf16)
+                    (packed[k : k + 1, :] == row_of).astype(f32).astype(bf16)
                     for k in range(take_blocks * batch)
                 ],
                 axis=1,
             )
-            finish(number, mul(picker, held[: take_blocks * batch * wide, :]))
+            return mul(picker, rows_held)
+
+        def step(number, carry):
+            finish(number - 1)
+            grads_ref[...] = gather(number)
+            leave(number - 1).start()
             return carry
 
-        lax.fori_loop(0, rows_dev // part, one_part, 0)
+        grads_ref[...] = gather(0)
+        lax.fori_loop(1, parts, step, 0)
 
     first = max(1, total_blocks // 2)
     for take_blocks in range(first, total_blocks + 1):
         chosen = blocks <= first if take_blocks == first else blocks == take_blocks
         pl.when(chosen)(partial(with_blocks, take_blocks))
 
-    for number in range(rows_dev // part):
+    finish(parts - 1)
+    leave(parts - 1).start()
+    for number in range(parts):
         new_state_ref[number * per_part : (number + 1) * per_part, :] = jnp.transpose(
             turned_new[number]
         )[:per_part]
+    for number in range(parts):
+        leave(number).wait()
 
 
 def update(asked, returned, table, state):
@@ -342,7 +361,7 @@
     rows_dev, features = table.shape
     wide = pl.cdiv(stride, lanes) * lanes
     part = min(512, rows_dev)
-    kept = pl.cdiv(peers, batch) * batch * wide
+    parts = rows_dev // part
     new_table, new_state = pl.pallas_call(
         update_kernel,
         out_shape=(
@@ -350,12 +369,15 @@
             jax.ShapeDtypeStruct((rows_dev // lanes, lanes), f32),
         ),
         in_specs=[in_smem, in_vmem, in_vmem, in_vmem, in_vmem],
-        out_specs=(in_vmem, in_vmem),
+        out_specs=(pl.BlockSpec(memory_space=pl.ANY), in_vmem),
         scratch_shapes=active_scratch(peers, stride)
         + [
-            pltpu.VMEM((kept, features), bf16),
-            pltpu.VMEM((rows_dev // part, lanes, lanes), f32),
-            pltpu.VMEM((rows_dev // part, lanes, lanes), f32),
+            pltpu.VMEM((pl.cdiv(peers, batch) * batch, wide, features), bf16),
+            pltpu.VMEM((parts, lanes, lanes), f32),
+            pltpu.VMEM((parts, lanes, lanes), f32),
+            pltpu.VMEM((part, features), f32),
+            pltpu.VMEM(table.shape, f32),
+            pltpu.SemaphoreType.DMA((parts,)),
         ],
         compiler_params=params(48),
         name="update",
@@ -379,12 +401,11 @@
     group_len = lhs_row.shape[2]
     peers = lax.axis_size("dom") * lax.axis_size("group")
     cap = pl.cdiv(5 * group_len // (4 * peers), 8) * 8
-    limit = jnp.clip(edge_count - lax.axis_index("group") * group_len, 0, group_len)
     indices = [
         x.reshape(1, group_len)
         for x in (lhs_owner, lhs_row, rhs_owner, rhs_row, neg_owner, neg_row)
     ]
-    ask, spots, fill = prep(limit, indices, peers, cap, rows_dev)
+    ask, spots, fill, limit = prep(edge_count, indices, peers, cap, rows_dev)
     asked = lax.all_to_all(ask, axes, split_axis=0, concat_axis=0, tiled=True)
     answer = fetch(asked, embeddings.astype(bf16))
     arrived = lax.all_to_all(answer, axes, split_axis=0, concat_axis=0, tiled=True)

time: 150 us -> 146 us (0.973); the launches traced: 147 us -> 146 us
  Pallas kernels: 31.1 us -> 29.5 us
    pallas_call x1, Pallas kernels: 13.9 us -> 10.3 us  [update(): pl.pallas_call(update_kernel, out_shape=(jax.ShapeDtypeStruct(table.shape...]
where the time goes in v2:
time: 146 us
  blocking collectives  96.9 us (66%)
  Pallas kernels  29.5 us (20%)
  starting transfers between devices  7.3 us (5%)
  waiting for transfers between devices  4.68 us (3%)
  local copies, waits for them, and re-layouts  4.12 us (3%)
  other arithmetic  2.39 us (2%)
  between operations  1.52 us (1%)
    all_to_all x1, blocking collectives, body(): lax.all_to_all(grads, axes, split_axis=0, concat_axis=0, tiled=True)  49.2 us
    all_to_all x1, blocking collectives, body(): lax.all_to_all(answer, axes, split_axis=0, concat_axis=0, tiled=True)  47.6 us
    pallas_call x1, Pallas kernels, update(): pl.pallas_call(update_kernel, out_shape=(jax.ShapeDtypeStruct(table.shape...  10.3 us
    pallas_call x1, Pallas kernels, train(): pl.pallas_call(train_kernel, out_shape=jax.ShapeDtypeStruct(arrived.shape...  9.13 us
    pallas_call x1, Pallas kernels, fetch(): pl.pallas_call(fetch_kernel, out_shape=jax.ShapeDtypeStruct((peers, strid...  7.32 us
    all_to_all x1, starting transfers between devices, body(): asked = lax.all_to_all(ask, axes, split_axis=0, concat_axis=0, tiled=True)  7.3 us
    all_to_all x1, waiting for transfers between devices, body(): asked = lax.all_to_all(ask, axes, split_axis=0, concat_axis=0, tiled=True)  4.68 us
    unnamed x16, local copies, waits for them, and re-layouts  4.12 us
  transfers between devices with their start and end apart: 1, of which 1 were waited for; matrix products, arithmetic and copies ran while one was open for 2% of the time, Pallas kernels for 0%

profile of v2, /device:TPU:0, one launch (start us, length us, event | category | flops | bytes accessed | tf_op | source)
XLA Modules:
  0.0 146.4 jit_solution(14171936700651573360)
XLA Ops:
  1.3 0.0 copy-start.2
  1.3 0.7 copy-done.2
  2.0 0.0 copy-start.3
  2.0 0.7 copy-done.3
  2.7 0.0 copy-start.4
  2.7 0.7 copy-done.4
  3.3 0.0 copy-start.5
  3.3 0.7 copy-done.5
  4.0 0.0 copy-start.6
  4.0 0.7 copy-done.6
  4.7 0.0 copy-start.7
  4.7 0.7 copy-done.7
  5.4 2.7 %prep.1 = (s32[32,120]{1,0:T(8,128)}, f32[8,1024]{1,0:T(8,128)S(1)}, f32[8,1280]{1,0:T(8,128)S(1)}, s32[1]{0:T(128)}) custom-call(s32[1]{0:T(128)S(6)} %copy.12.count_hbm, s32[1,1024]{1,0:T(1,128)S(1)} %bitcast.17, s32[1,1024]{1,0:T(1,128)S(1)} %bitcast.18, s32[1,1024]{1,0:T(1,128)S(1)} %bitcast.19, s32[1,1024]{1,0:T(1,128)S(1)} %bitcast.20, ...), custom_call_target="tpu_custom_call" | custom-call | tf_op jit(solution)/shard_map/prep/pallas_call | solution.py:93
  8.1 7.3 %all-to-all-start = ((s32[32,1,120]{2,1,0:T(1,128)}), s32[32,1,120]{2,1,0:T(1,128)S(1)}, u32[]{:S(2)}, u32[]{:S(2)}) async-start(s32[32,1,120]{2,1,0:T(1,128)} %bitcast.7), calls=%async_computation | async-start | bytes 32768 | tf_op jit(solution)/shard_map/all_to_all | solution.py:409
  15.4 2.4 %convert_element_type.3.table_ref = bf16[4096,256]{1,0:T(8,128)(2,1)S(1)} convert(f32[4096,256]{1,0:T(8,128)} %table_ref.1) | non-fusion elementwise | flops 1048576 | bytes 6291456 | tf_op jit(solution)/shard_map/convert_element_type | solution.py:410
  17.8 4.7 %all-to-all-done = s32[32,1,120]{2,1,0:T(1,128)S(1)} async-done(((s32[32,1,120]{2,1,0:T(1,128)}), s32[32,1,120]{2,1,0:T(1,128)S(1)}, u32[]{:S(2)}, u32[]{:S(2)}) %all-to-all-start) | async-done | bytes 15392 | tf_op jit(solution)/shard_map/all_to_all | solution.py:409
  22.5 7.3 %fetch.1 = bf16[32,120,256]{2,1,0:T(8,128)(2,1)S(1)} custom-call(s32[32,120]{1,0:T(8,128)S(1)} %bitcast.12, s32[32,120]{1,0:T(8,128)S(1)} %bitcast.13, bf16[4096,256]{1,0:T(8,128)(2,1)S(1)} %convert_element_type.3.table_ref), custom_call_target="tpu_custom_call" | custom-call | tf_op jit(solution)/shard_map/fetch/pallas_call | solution.py:155
  29.8 47.6 %all_to_all.21.come_ref = bf16[32,120,256]{2,1,0:T(8,128)(2,1)S(1)} all-to-all(bf16[32,120,256]{2,1,0:T(8,128)(2,1)S(1)} %fetch.1), channel_id=1, replica_groups=mesh['dom'=8,'group'=4] {'dom','group'}, dimensions={0} | all-to-all | bytes 3932160 | tf_op jit(solution)/shard_map/all_to_all | solution.py:411
  77.5 0.0 copy-start
  77.5 9.1 %train.1 = bf16[32,120,256]{2,1,0:T(8,128)(2,1)S(1)} custom-call(s32[1]{0:T(128)} %get-tuple-element.9.limit_ref, f32[8,1024]{1,0:T(8,128)S(1)} %get-tuple-element.10.spot_ref, f32[8,1280]{1,0:T(8,128)S(1)} %get-tuple-element.11.fill_ref, bf16[32,120,256]{2,1,0:T(8,128)(2,1)S(1)} %all_to_all.21.come_ref), custom_call_target="tpu_custom_call" | custom-call | tf_op jit(solution)/shard_map/train/pallas_call | solution.py:256
  86.6 0.0 copy-start.1
  86.6 49.2 %all_to_all.22.back_ref = bf16[32,120,256]{2,1,0:T(8,128)(2,1)S(1)} all-to-all(bf16[32,120,256]{2,1,0:T(8,128)(2,1)S(1)} %train.1), channel_id=1, replica_groups=mesh['dom'=8,'group'=4] {'dom','group'}, dimensions={0} | all-to-all | bytes 3932160 | tf_op jit(solution)/shard_map/all_to_all | solution.py:413
  135.9 0.0 copy-done
  135.9 0.0 copy-done.1
  135.9 10.3 %update.1 = (f32[4096,256]{1,0:T(8,128)}, f32[32,128]{1,0:T(8,128)}) custom-call(s32[32,120]{1,0:T(8,128)S(1)} %bitcast.14, s32[32,120]{1,0:T(8,128)S(1)} %bitcast.15, bf16[32,120,256]{2,1,0:T(8,128)(2,1)S(1)} %all_to_all.22.back_ref, f32[4096,256]{1,0:T(8,128)S(1)} %copy-done, f32[32,128]{1,0:T(8,128)S(1)} %bitcast.16), custom_call_target="tpu_custom_call" | custom-call | tf_op jit(solution)/shard_map/update/pallas_call | solution.py:365
Async XLA Ops:
  1.3 0.7 copy-start.2
  2.0 0.7 copy-start.3
  2.7 0.7 copy-start.4
  3.3 0.7 copy-start.5
  4.0 0.7 copy-start.6
  4.7 0.7 copy-start.7
  8.1 14.4 %all-to-all-start = ((s32[32,1,120]{2,1,0:T(1,128)}), s32[32,1,120]{2,1,0:T(1,128)S(1)}, u32[]{:S(2)}, u32[]{:S(2)}) async-start(s32[32,1,120]{2,1,0:T(1,128)} %bitcast.7), calls=%async_computation | async-start | bytes 32768 | tf_op jit(solution)/shard_map/all_to_all | solution.py:409
  77.5 58.4 %copy-start = (f32[4096,256]{1,0:T(8,128)S(1)}, f32[4096,256]{1,0:T(8,128)}, u32[]{:S(2)}) copy-start(f32[4096,256]{1,0:T(8,128)} %table_ref.1) | copy-start | bytes 12582916
  86.6 49.3 %copy-start.1 = (f32[4096]{0:T(1024)S(1)}, f32[4096]{0:T(1024)}, u32[]{:S(2)}) copy-start(f32[4096]{0:T(1024)} %param.10) | copy-start | bytes 49156

commit v3 on v2

--- a/solution.py
+++ b/solution.py
@@ -12,7 +12,7 @@
 lanes = 128
 batch = 4
 in_vmem = pl.BlockSpec(memory_space=pltpu.VMEM)
-in_smem = pl.BlockSpec(memory_space=pltpu.SMEM)
+in_hbm = pl.BlockSpec(memory_space=pltpu.HBM)
 by_rows = (((1,), (1,)), ((), ()))
 f32, bf16, i32 = jnp.float32, jnp.bfloat16, jnp.int32
 
@@ -36,8 +36,8 @@
 def prep_kernel(
     rows_dev, count_hbm, *refs
 ):
-    index_hbm, (ask_ref, spot_ref, fill_ref, limit_ref) = refs[:6], refs[6:10]
-    index_refs, edges, arrivals = refs[10:16], refs[16], refs[17]
+    index_hbm, (ask_ref, spot_ref, fill_ref) = refs[:6], refs[6:9]
+    index_refs, edges, arrivals = refs[9:15], refs[15], refs[16]
     copies = [
         pltpu.make_async_copy(source, target, arrivals.at[number])
         for number, (source, target) in enumerate(
@@ -58,7 +58,7 @@
     for copy in copies:
         copy.wait()
     limit = jnp.clip(edges[0] - lax.axis_index("group") * count, 0, count)
-    limit_ref[0] = limit
+    spot_ref[3:4, :] = jnp.full((1, count), limit, i32).astype(f32)
     for kind in range(3):
         owner = index_refs[2 * kind][...]
         row = index_refs[2 * kind + 1][...]
@@ -89,41 +89,43 @@
 
 def prep(edge_count, indices, peers, cap, rows_dev):
     count = indices[0].shape[1]
-    anywhere = pl.BlockSpec(memory_space=pl.ANY)
     return pl.pallas_call(
         partial(prep_kernel, rows_dev),
         out_shape=(
             jax.ShapeDtypeStruct((peers, 3 * cap), i32),
             jax.ShapeDtypeStruct((8, count), f32),
             jax.ShapeDtypeStruct((8, peers * cap), f32),
-            jax.ShapeDtypeStruct((1,), i32),
         ),
-        in_specs=[anywhere] * 7,
-        out_specs=(in_vmem, in_vmem, in_vmem, in_smem),
+        in_specs=[in_hbm] * 7,
+        out_specs=(in_vmem, in_vmem, in_vmem),
         scratch_shapes=[pltpu.VMEM((1, count), i32)] * 6
         + [pltpu.SMEM((1,), i32), pltpu.SemaphoreType.DMA((7,))],
-        compiler_params=params(32),
+        compiler_params=params(62),
         name="prep",
     )(edge_count, *indices)
 
 
-def pack_active(asked_s, asked_v, who, packed):
-    peers, stride = asked_v.shape
+def pack_active(asked_ref, who, packed):
+    peers, stride = asked_ref.shape
+    bits = 16
+    flags = (asked_ref[:, 0:1] >= 0).astype(f32)
+    flags = flags * (1 << iota((peers, 1), 0) % bits).astype(f32)
+    words = [jnp.sum(flags[k : k + bits]).astype(i32) for k in range(0, peers, bits)]
     packed[...] = jnp.full(packed.shape, -1, i32)
     used = 0
     for peer in range(peers):
         who[used] = peer
-        packed[pl.ds(used, 1), :stride] = asked_v[peer : peer + 1, :]
-        used = used + (asked_s[peer, 0] >= 0).astype(i32)
+        packed[pl.ds(used, 1), :stride] = asked_ref[peer : peer + 1, :]
+        used = used + ((words[peer // bits] >> (peer % bits)) & 1)
     packed[pl.ds(used, 1), :] = jnp.full((1, packed.shape[1]), -1, i32)
     return used
 
 
-def fetch_kernel(asked_s, asked_v, table_ref, out_ref, who, packed):
-    stride = asked_v.shape[1]
+def fetch_kernel(asked_ref, table_ref, out_ref, who, packed):
+    stride = asked_ref.shape[1]
     wide = packed.shape[1]
     rows_dev = table_ref.shape[0]
-    used = pack_active(asked_s, asked_v, who, packed)
+    used = pack_active(asked_ref, who, packed)
     row_of = iota((wide, rows_dev), 1)
 
     def block(first, size):
@@ -155,16 +157,16 @@
     return pl.pallas_call(
         fetch_kernel,
         out_shape=jax.ShapeDtypeStruct((peers, stride, table.shape[1]), bf16),
-        in_specs=[in_smem, in_vmem, in_vmem],
+        in_specs=[in_vmem, in_vmem],
         out_specs=in_vmem,
         scratch_shapes=active_scratch(peers, stride),
         compiler_params=params(40),
         name="fetch",
-    )(asked, asked, table)
+    )(asked, table)
 
 
 def train_kernel(
-    limit_ref, spot_ref, fill_ref, come_ref, go_ref, wide_ref, place_ref, left_ref, right_ref,
+    spot_ref, fill_ref, come_ref, go_ref, wide_ref, place_ref, left_ref, right_ref, live_ref,
     gl_ref, pg_ref, ps_ref, pr_ref
 ):
     peers, stride, features = come_ref.shape
@@ -172,95 +174,83 @@
     slots = peers * cap
     count = spot_ref.shape[1]
     part = min(256, count)
-    limit = limit_ref[0]
-
-    @pl.when(limit > 0)
-    def active():
-        def split(peer, carry):
-            rows = come_ref[peer].astype(f32)
-            for kind in range(3):
-                wide_ref[kind, pl.ds(pl.multiple_of(peer * cap, 8), cap), :] = rows[
-                    kind * cap : kind * cap + cap
-                ]
-            return carry
-
-        lax.fori_loop(0, peers, split, 0)
-        spot_rows = spot_ref[...]
-        spot_columns = jnp.transpose(spot_rows)
-        slot_across = iota((part, slots), 1).astype(f32)
-        for kind, target in ((0, left_ref), (1, right_ref)):
-            held = wide_ref[kind].astype(bf16)
-            for start in range(0, count, part):
-                column = spot_columns[start : start + part, kind : kind + 1]
-                picker = (column == slot_across).astype(f32).astype(bf16)
-                target[start : start + part, :] = mul(picker, held).astype(bf16)
-        shared_rows = wide_ref[2].astype(bf16)
-        fill = fill_ref[0:1, :]
-        off_diagonal = (iota((part, part), 0) != iota((part, part), 1)).astype(f32)
-        for start in range(0, count, part):
-            here = slice(start, start + part)
-            left = left_ref[here, :]
-            left_wide = left.astype(f32)
-            right_wide = right_ref[here, :].astype(f32)
-            pos_exp = jnp.exp(jnp.sum(left_wide * right_wide, axis=1, keepdims=True))
-            shared_exp = jnp.exp(mul_t(left, shared_rows)) * fill
-            total = pos_exp + jnp.sum(shared_exp, axis=1, keepdims=True)
-            chunk_exps = []
-            for other in range(0, count, part):
-                chunk_exp = jnp.exp(mul_t(left, right_ref[other : other + part, :]))
-                chunk_exp = chunk_exp * (iota((1, part), 1) + other < limit).astype(f32)
-                if other == start:
-                    chunk_exp = chunk_exp * off_diagonal
-                total = total + jnp.sum(chunk_exp, axis=1, keepdims=True)
-                chunk_exps.append(chunk_exp)
-            live = (iota((part, 1), 0) + start < limit).astype(f32)
-            weight = live / total
-            pos_grad = live * (pos_exp / total - 1.0)
-            shared_prob = (shared_exp * weight).astype(bf16)
-            ps_ref[here, :] = shared_prob
-            grad = pos_grad * right_wide + mul(shared_prob, shared_rows)
-            for other, chunk_exp in zip(range(0, count, part), chunk_exps):
-                chunk_prob = (chunk_exp * weight).astype(bf16)
-                pr_ref[here, other : other + part] = chunk_prob
-                grad = grad + mul(chunk_prob, right_ref[other : other + part, :])
-            gl_ref[here, :] = grad.astype(bf16)
-            pg_ref[here, :] = pos_grad * left_wide
-        left_turned = jnp.transpose(left_ref[...].astype(f32)).astype(bf16)
-        place_ref[2] = jnp.transpose(mul(left_turned, ps_ref[...]))
-        grad_right = jnp.transpose(mul(left_turned, pr_ref[...])) + pg_ref[...]
-        right_ref[...] = grad_right.astype(bf16)
-        slot_down = iota((part, count), 0).astype(f32)
-        for kind, source in ((0, gl_ref), (1, right_ref)):
-            for start in range(0, slots, part):
-                picker = (spot_rows[kind : kind + 1, :] - float(start) == slot_down)
-                picker = picker.astype(f32).astype(bf16)
-                place_ref[kind, start : start + part, :] = mul(picker, source[...])
-
-        def join(peer, carry):
-            go_ref[peer] = jnp.concatenate(
-                [
-                    place_ref[kind, pl.ds(pl.multiple_of(peer * cap, 8), cap), :]
-                    for kind in range(3)
-                ],
-                axis=0,
-            ).astype(bf16)
-            return carry
-
-        lax.fori_loop(0, peers, join, 0)
-
-
-def train(limit, spots, fill, arrived):
+    starts = range(0, count, part)
+    for peer in range(peers):
+        rows = come_ref[peer].astype(f32)
+        for kind in range(3):
+            wide_ref[kind, peer * cap : peer * cap + cap, :] = rows[kind * cap : kind * cap + cap]
+    spot_rows = spot_ref[...]
+    spot_columns = jnp.transpose(spot_rows)
+    limit = spot_rows[3:4, 0:1]
+    live_across = (iota((1, count), 1).astype(f32) < limit).astype(f32)
+    live_down = (iota((count, 1), 0).astype(f32) < limit).astype(f32)
+    slot_across = iota((part, slots), 1).astype(f32)
+    for kind, target in ((0, left_ref), (1, right_ref)):
+        held = wide_ref[kind].astype(bf16)
+        for start in starts:
+            column = spot_columns[start : start + part, kind : kind + 1]
+            picker = (column == slot_across).astype(f32).astype(bf16)
+            rows = mul(picker, held)
+            target[start : start + part, :] = rows.astype(bf16)
+            if kind == 1:
+                rows = rows * live_down[start : start + part]
+                live_ref[start : start + part, :] = rows.astype(bf16)
+    shared_rows = wide_ref[2].astype(bf16)
+    fill = fill_ref[0:1, :]
+    off_diagonal = (iota((part, part), 0) != iota((part, part), 1)).astype(f32)
+    for start in starts:
+        here = slice(start, start + part)
+        left = left_ref[here, :]
+        left_wide = left.astype(f32)
+        right_wide = right_ref[here, :].astype(f32)
+        pos_exp = jnp.exp(jnp.sum(left_wide * right_wide, axis=1, keepdims=True))
+        shared_exp = jnp.exp(mul_t(left, shared_rows))
+        total = pos_exp + jnp.sum(shared_exp * fill, axis=1, keepdims=True)
+        chunk_exps = []
+        for other in starts:
+            chunk_exp = jnp.exp(mul_t(left, right_ref[other : other + part, :]))
+            if other == start:
+                chunk_exp = chunk_exp * off_diagonal
+            counted = chunk_exp * live_across[:, other : other + part]
+            total = total + jnp.sum(counted, axis=1, keepdims=True)
+            chunk_exps.append(chunk_exp)
+        live = live_down[here]
+        weight = live / total
+        pos_grad = live * (pos_exp / total - 1.0)
+        ps_ref[here, :] = (shared_exp * weight).astype(bf16)
+        for other, chunk_exp in zip(starts, chunk_exps):
+            pr_ref[here, other : other + part] = (chunk_exp * weight).astype(bf16)
+        pull = mul(ps_ref[here, :], shared_rows) + mul(pr_ref[here, :], live_ref[...])
+        gl_ref[here, :] = (pos_grad * right_wide + pull).astype(bf16)
+        pg_ref[here, :] = pos_grad * left_wide
+    left_turned = jnp.transpose(left_ref[...].astype(f32)).astype(bf16)
+    place_ref[2] = jnp.transpose(mul(left_turned, ps_ref[...]))
+    grad_right = jnp.transpose(mul(left_turned, pr_ref[...])) * live_down + pg_ref[...]
+    right_ref[...] = grad_right.astype(bf16)
+    slot_down = iota((part, count), 0).astype(f32)
+    for kind, source in ((0, gl_ref), (1, right_ref)):
+        for start in range(0, slots, part):
+            picker = spot_rows[kind : kind + 1, :] - float(start) == slot_down
+            picker = picker.astype(f32).astype(bf16)
+            place_ref[kind, start : start + part, :] = mul(picker, source[...])
+    for peer in range(peers):
+        rows = [place_ref[kind, peer * cap : peer * cap + cap, :] for kind in range(3)]
+        go_ref[peer] = jnp.concatenate(rows, axis=0).astype(bf16)
+
+
+def train(spots, fill, arrived):
     peers, stride, features = arrived.shape
     count = spots.shape[1]
     slots = fill.shape[1]
     return pl.pallas_call(
         train_kernel,
         out_shape=jax.ShapeDtypeStruct(arrived.shape, bf16),
-        in_specs=[in_smem, in_vmem, in_vmem, in_vmem],
+        in_specs=[in_vmem, in_vmem, in_vmem],
         out_specs=in_vmem,
         scratch_shapes=[
             pltpu.VMEM((3, slots, features), f32),
             pltpu.VMEM((3, slots, features), f32),
+            pltpu.VMEM((count, features), bf16),
             pltpu.VMEM((count, features), bf16),
             pltpu.VMEM((count, features), bf16),
             pltpu.VMEM((count, features), bf16),
@@ -270,21 +260,21 @@
         ],
         compiler_params=params(48),
         name="train",
-    )(limit, spots, fill, arrived)
+    )(spots, fill, arrived)
 
 
 def update_kernel(
-    asked_s, asked_v, back_ref, table_ref, state_ref, out_hbm, new_state_ref, who, packed, held,
+    asked_ref, back_ref, table_ref, state_ref, out_hbm, new_state_ref, who, packed, held,
     turned, turned_new, grads_ref, out_ref, left
 ):
-    peers, stride = asked_v.shape
+    peers, stride = asked_ref.shape
     wide = packed.shape[1]
     rows_dev, features = table_ref.shape
     total_blocks = pl.cdiv(peers, batch)
     part = min(512, rows_dev)
     parts = rows_dev // part
     per_part = part // lanes
-    used = pack_active(asked_s, asked_v, who, packed)
+    used = pack_active(asked_ref, who, packed)
     blocks = pl.cdiv(used, batch)
     if wide > stride:
         tail = stride // 16 * 16
@@ -368,8 +358,8 @@
             jax.ShapeDtypeStruct(table.shape, f32),
             jax.ShapeDtypeStruct((rows_dev // lanes, lanes), f32),
         ),
-        in_specs=[in_smem, in_vmem, in_vmem, in_vmem, in_vmem],
-        out_specs=(pl.BlockSpec(memory_space=pl.ANY), in_vmem),
+        in_specs=[in_vmem, in_vmem, in_vmem, in_vmem],
+        out_specs=(in_hbm, in_vmem),
         scratch_shapes=active_scratch(peers, stride)
         + [
             pltpu.VMEM((pl.cdiv(peers, batch) * batch, wide, features), bf16),
@@ -381,7 +371,7 @@
         ],
         compiler_params=params(48),
         name="update",
-    )(asked, asked, returned, table, state.reshape(rows_dev // lanes, lanes))
+    )(asked, returned, table, state.reshape(rows_dev // lanes, lanes))
     return new_table, new_state.reshape(rows_dev)
 
 
@@ -405,11 +395,11 @@
         x.reshape(1, group_len)
         for x in (lhs_owner, lhs_row, rhs_owner, rhs_row, neg_owner, neg_row)
     ]
-    ask, spots, fill, limit = prep(edge_count, indices, peers, cap, rows_dev)
+    ask, spots, fill = prep(edge_count, indices, peers, cap, rows_dev)
     asked = lax.all_to_all(ask, axes, split_axis=0, concat_axis=0, tiled=True)
     answer = fetch(asked, embeddings.astype(bf16))
     arrived = lax.all_to_all(answer, axes, split_axis=0, concat_axis=0, tiled=True)
-    grads = train(limit, spots, fill, arrived)
+    grads = train(spots, fill, arrived)
     returned = lax.all_to_all(grads, axes, split_axis=0, concat_axis=0, tiled=True)
     return update(asked, returned, embeddings, adagrad_state)
 

time: 146 us -> 142 us (0.973)
  local copies, waits for them, and re-layouts: 4.12 us -> 0.02 us
    unnamed x16 -> x8, local copies, waits for them, and re-layouts: 4.12 us -> 0.02 us
    pallas_call x1, Pallas kernels: 9.13 us -> 7.62 us  [train(): pl.pallas_call(train_kernel, out_shape=jax.ShapeDtypeStruct(arrived.shape...]
where the time goes in v3:
time: 142 us
  blocking collectives  96.9 us (68%)
  Pallas kernels  29 us (20%)
  starting transfers between devices  7.3 us (5%)
  waiting for transfers between devices  4.68 us (3%)
  other arithmetic  2.39 us (2%)
  between operations  1.52 us (1%)
    all_to_all x1, blocking collectives, body(): lax.all_to_all(grads, axes, split_axis=0, concat_axis=0, tiled=True)  49.2 us
    all_to_all x1, blocking collectives, body(): lax.all_to_all(answer, axes, split_axis=0, concat_axis=0, tiled=True)  47.6 us
    pallas_call x1, Pallas kernels, update(): pl.pallas_call(update_kernel, out_shape=(jax.ShapeDtypeStruct(table.shape...  10.7 us
    pallas_call x1, Pallas kernels, fetch(): pl.pallas_call(fetch_kernel, out_shape=jax.ShapeDtypeStruct((peers, strid...  7.77 us
    pallas_call x1, Pallas kernels, train(): pl.pallas_call(train_kernel, out_shape=jax.ShapeDtypeStruct(arrived.shape...  7.62 us
    all_to_all x1, starting transfers between devices, body(): asked = lax.all_to_all(ask, axes, split_axis=0, concat_axis=0, tiled=True)  7.3 us
    all_to_all x1, waiting for transfers between devices, body(): asked = lax.all_to_all(ask, axes, split_axis=0, concat_axis=0, tiled=True)  4.68 us
    pallas_call x1, Pallas kernels, prep(): pl.pallas_call(partial(prep_kernel, rows_dev), out_shape=(jax.ShapeDtypeS...  2.89 us
  transfers between devices with their start and end apart: 1, of which 1 were waited for; matrix products, arithmetic and copies ran while one was open for 2% of the time, Pallas kernels for 0%

profile of v3, /device:TPU:0, one launch (start us, length us, event | category | flops | bytes accessed | tf_op | source)
XLA Modules:
  0.0 141.8 jit_solution(3681036811526877433)
XLA Ops:
  1.3 2.9 %prep.1 = (s32[32,120]{1,0:T(8,128)}, f32[8,1024]{1,0:T(8,128)}, f32[8,1280]{1,0:T(8,128)}) custom-call(s32[1]{0:T(128)S(6)} %copy.12.count_hbm, s32[1,1024]{1,0:T(1,128)} %bitcast.16, s32[1,1024]{1,0:T(1,128)} %bitcast.17, s32[1,1024]{1,0:T(1,128)} %bitcast.18, s32[1,1024]{1,0:T(1,128)} %bitcast.19, s32[1,1024]{1,0:T(1,128)} %bitcast.20, s32[1,1024]{1,0:T(1,128)} %bitcast.21), custom_call_target="tpu_custom_call" | custom-call | tf_op jit(solution)/shard_map/prep/pallas_call | solution.py:92
  4.2 7.3 %all-to-all-start = ((s32[32,1,120]{2,1,0:T(1,128)}), s32[32,1,120]{2,1,0:T(1,128)S(1)}, u32[]{:S(2)}, u32[]{:S(2)}) async-start(s32[32,1,120]{2,1,0:T(1,128)} %bitcast.15), calls=%async_computation | async-start | bytes 32768 | tf_op jit(solution)/shard_map/all_to_all | solution.py:399
  11.5 2.4 %convert_element_type.3.table_ref = bf16[4096,256]{1,0:T(8,128)(2,1)S(1)} convert(f32[4096,256]{1,0:T(8,128)} %table_ref.1) | non-fusion elementwise | flops 1048576 | bytes 6291456 | tf_op jit(solution)/shard_map/convert_element_type | solution.py:400
  13.9 4.7 %all-to-all-done = s32[32,1,120]{2,1,0:T(1,128)S(1)} async-done(((s32[32,1,120]{2,1,0:T(1,128)}), s32[32,1,120]{2,1,0:T(1,128)S(1)}, u32[]{:S(2)}, u32[]{:S(2)}) %all-to-all-start) | async-done | bytes 15392 | tf_op jit(solution)/shard_map/all_to_all | solution.py:399
  18.6 7.8 %fetch.1 = bf16[32,120,256]{2,1,0:T(8,128)(2,1)S(1)} custom-call(s32[32,120]{1,0:T(8,128)S(1)} %bitcast.12, bf16[4096,256]{1,0:T(8,128)(2,1)S(1)} %convert_element_type.3.table_ref), custom_call_target="tpu_custom_call" | custom-call | tf_op jit(solution)/shard_map/fetch/pallas_call | solution.py:157
  26.3 0.0 copy-start.1
  26.4 0.0 copy-start.2
  26.4 47.6 %all_to_all.21.come_ref = bf16[32,120,256]{2,1,0:T(8,128)(2,1)S(1)} all-to-all(bf16[32,120,256]{2,1,0:T(8,128)(2,1)S(1)} %fetch.1), channel_id=1, replica_groups=mesh['dom'=8,'group'=4] {'dom','group'}, dimensions={0} | all-to-all | bytes 3932160 | tf_op jit(solution)/shard_map/all_to_all | solution.py:401
  74.0 0.0 copy-done.1
  74.0 0.0 copy-done.2
  74.0 0.0 copy-start
  74.0 7.6 %train.1 = bf16[32,120,256]{2,1,0:T(8,128)(2,1)S(1)} custom-call(f32[8,1024]{1,0:T(8,128)S(1)} %copy-done.2, f32[8,1280]{1,0:T(8,128)S(1)} %copy-done.1, bf16[32,120,256]{2,1,0:T(8,128)(2,1)S(1)} %all_to_all.21.come_ref), custom_call_target="tpu_custom_call" | custom-call | tf_op jit(solution)/shard_map/train/pallas_call | solution.py:245
  81.6 0.0 copy-start.3
  81.6 49.2 %all_to_all.22.back_ref = bf16[32,120,256]{2,1,0:T(8,128)(2,1)S(1)} all-to-all(bf16[32,120,256]{2,1,0:T(8,128)(2,1)S(1)} %train.1), channel_id=1, replica_groups=mesh['dom'=8,'group'=4] {'dom','group'}, dimensions={0} | all-to-all | bytes 3932160 | tf_op jit(solution)/shard_map/all_to_all | solution.py:403
  130.9 0.0 copy-done
  130.9 0.0 copy-done.3
  130.9 10.7 %update.1 = (f32[4096,256]{1,0:T(8,128)}, f32[32,128]{1,0:T(8,128)}) custom-call(s32[32,120]{1,0:T(8,128)S(1)} %bitcast.13, bf16[32,120,256]{2,1,0:T(8,128)(2,1)S(1)} %all_to_all.22.back_ref, f32[4096,256]{1,0:T(8,128)S(1)} %copy-done, f32[32,128]{1,0:T(8,128)S(1)} %bitcast.14), custom_call_target="tpu_custom_call" | custom-call | tf_op jit(solution)/shard_map/update/pallas_call | solution.py:355
Async XLA Ops:
  4.2 14.4 %all-to-all-start = ((s32[32,1,120]{2,1,0:T(1,128)}), s32[32,1,120]{2,1,0:T(1,128)S(1)}, u32[]{:S(2)}, u32[]{:S(2)}) async-start(s32[32,1,120]{2,1,0:T(1,128)} %bitcast.15), calls=%async_computation | async-start | bytes 32768 | tf_op jit(solution)/shard_map/all_to_all | solution.py:399
  26.3 47.6 %copy-start.1 = (f32[8,1280]{1,0:T(8,128)S(1)}, f32[8,1280]{1,0:T(8,128)}, u32[]{:S(2)}) copy-start(f32[8,1280]{1,0:T(8,128)} %get-tuple-element.9.fill_ref) | copy-start | bytes 122884
  26.4 47.6 %copy-start.2 = (f32[8,1024]{1,0:T(8,128)S(1)}, f32[8,1024]{1,0:T(8,128)}, u32[]{:S(2)}) copy-start(f32[8,1024]{1,0:T(8,128)} %get-tuple-element.8.spot_ref) | copy-start | bytes 98308
  74.0 56.9 %copy-start = (f32[4096,256]{1,0:T(8,128)S(1)}, f32[4096,256]{1,0:T(8,128)}, u32[]{:S(2)}) copy-start(f32[4096,256]{1,0:T(8,128)} %table_ref.1) | copy-start | bytes 12582916
  81.6 49.3 %copy-start.3 = (f32[4096]{0:T(1024)S(1)}, f32[4096]{0:T(1024)}, u32[]{:S(2)}) copy-start(f32[4096]{0:T(1024)} %param.10) | copy-start | bytes 49156

commit v4 on v3

v4 whole, which is shorter than its diff:
```python
from functools import partial

import jax
import jax.numpy as jnp
from jax import lax
from jax.experimental import pallas as pl
from jax.experimental.pallas import tpu as pltpu
from jax.sharding import PartitionSpec as P

learn_rate = 0.1
adagrad_eps = 1e-06
lanes = 128
in_vmem = pl.BlockSpec(memory_space=pltpu.VMEM)
in_smem = pl.BlockSpec(memory_space=pltpu.SMEM)
in_hbm = pl.BlockSpec(memory_space=pltpu.HBM)
by_rows = (((1,), (1,)), ((), ()))
f32, bf16, i32 = jnp.float32, jnp.bfloat16, jnp.int32


def params(mib):
    return pltpu.CompilerParams(vmem_limit_bytes=mib * 2**20)


def mul(a, b):
    return jnp.dot(a, b, preferred_element_type=f32)


def mul_t(a, b):
    return lax.dot_general(a, b, by_rows, preferred_element_type=f32)


def iota(shape, dim):
    return lax.broadcasted_iota(i32, shape, dim)


def prep_kernel(rows_dev, wide, stride, count_hbm, *refs):
    index_hbm, message_ref = refs[:6], refs[6]
    index_refs, edges, arrivals = refs[7:13], refs[13], refs[14]
    copies = [
        pltpu.make_async_copy(source, target, arrivals.at[number])
        for number, (source, target) in enumerate(
            zip((count_hbm, *index_hbm), (edges, *index_refs))
        )
    ]
    for copy in copies:
        copy.start()
    peers = message_ref.shape[0]
    cap = stride // 3
    count = index_refs[0].shape[1]
    part = min(256, count)
    upper = (iota((part, part), 0) < iota((part, part), 1)).astype(f32).astype(bf16)
    peer_of = iota((peers, count), 0)
    slot_of = iota((wide, count), 0).astype(f32)
    for copy in copies:
        copy.wait()
    limit = jnp.clip(edges[0] - lax.axis_index("group") * count, 0, count)
    limit = jnp.full((1, 1), limit, i32)
    live = (iota((1, count), 1) < limit).astype(f32)
    active = (limit > 0).astype(f32)
    matches, ranks, sizes = [], [], []
    for kind in range(3):
        match = (index_refs[2 * kind][...] == peer_of).astype(f32)
        match = match * (active if kind == 2 else live)
        seen = jnp.zeros((peers, 1), f32)
        pieces = []
        for start in range(0, count, part):
            now = match[:, start : start + part]
            before = mul(now.astype(bf16), upper) + seen
            seen = seen + jnp.sum(now, axis=1, keepdims=True)
            pieces.append(jnp.sum(now * before, axis=0, keepdims=True))
        matches.append(match.astype(bf16))
        ranks.append(jnp.concatenate(pieces, axis=1))
        most = jnp.max(seen, axis=0, keepdims=True).astype(i32)
        sizes.append(((most + 7) // 8 * 8).astype(f32))
    starts = [jnp.zeros((1, 1), f32), sizes[0], sizes[0] + sizes[1]]
    high = low = there = jnp.zeros((peers, wide), f32)
    for kind in range(3):
        row = index_refs[2 * kind + 1][...]
        slot = (ranks[kind] + starts[kind] == slot_of).astype(f32)
        high += mul_t(matches[kind], (slot * (row // 64).astype(f32)).astype(bf16))
        low += mul_t(matches[kind], (slot * (row % 64).astype(f32)).astype(bf16))
        there += mul_t(matches[kind], slot.astype(bf16))
    said = jnp.where(there > 0.5, high * 64.0 + low, float(rows_dev))
    lane = iota((peers, wide), 1) - stride
    for number, value in enumerate((starts[2] + sizes[2], limit.astype(f32), starts[1], starts[2])):
        said = jnp.where(lane == number, value, said)
    said = said.astype(i32)
    shared = mul_t(jnp.ones((8, count), bf16), matches[2])[0:1, :]
    shared = shared.astype(i32)
    spots = [
        jnp.where(live > 0.5, index_refs[2 * kind][...].astype(f32) * cap + ranks[kind], 4095.0)
        for kind in range(2)
    ]
    spots = (spots[0] * 4096.0 + spots[1]).astype(i32)
    for peer in range(peers):
        message_ref[peer, :, :wide] = said[peer : peer + 1]
        message_ref[peer, :, wide : wide + peers] = shared
        message_ref[peer, :, message_ref.shape[2] - count :] = spots


def up_to_lanes(size):
    return pl.cdiv(size, lanes) * lanes


def prep(edge_count, indices, peers, stride, rows_dev):
    count = indices[0].shape[1]
    wide = up_to_lanes(stride + 8)
    return pl.pallas_call(
        partial(prep_kernel, rows_dev, wide, stride),
        out_shape=jax.ShapeDtypeStruct((peers, 1, wide + up_to_lanes(peers) + count), i32),
        in_specs=[pl.BlockSpec(memory_space=pl.ANY)] + [in_hbm] * 6,
        out_specs=in_vmem,
        scratch_shapes=[pltpu.VMEM((1, count), i32)] * 6
        + [pltpu.SMEM((1,), i32), pltpu.SemaphoreType.DMA((7,))],
        compiler_params=params(62),
        name="prep",
    )(edge_count, *indices)


def plan_kernel(sizes, wide, stride, rows_dev, got_ref, choice_ref, info_ref, rows_ref):
    peers = got_ref.shape[0]
    chips = peers // 2
    heads = got_ref[:, :wide]
    down = heads[:, stride : stride + 1].astype(f32)
    across = jnp.transpose(jnp.broadcast_to(down, (peers, lanes)))[0:1, :]
    u, t = iota((peers, peers), 0), iota((peers, peers), 1)
    ahead = (down > across) | ((down == across) & (u < t))
    rank = jnp.sum(ahead.astype(f32), axis=0, keepdims=True)
    chip = jnp.where(rank < chips, rank, peers - 1 - rank)
    held = (iota((chips, peers), 0).astype(f32) == chip).astype(f32) * across
    need = jnp.max(jnp.sum(held, axis=1, keepdims=True))
    choice = jnp.int32(0)
    for size in sizes[:-1]:
        choice = choice + (need > 2.0 * size).astype(i32)
    choice_ref[0] = choice
    alone = choice == len(sizes) - 1
    me = lax.axis_index("dom") * lax.axis_size("group") + lax.axis_index("group")
    mine = (me // 2).astype(f32)
    want = jnp.where(me % 2 == 0, mine, peers - 1 - mine)
    want = jnp.where(alone, me.astype(f32), want)
    place = iota((1, peers), 1).astype(f32)
    group = jnp.sum((rank == want).astype(f32) * place).astype(i32)
    first = jnp.sum((rank == mine).astype(f32) * across, axis=1, keepdims=True).astype(i32)
    size = jnp.int32(sizes[0])
    for number in range(1, len(sizes)):
        size = jnp.where(choice == number, sizes[number], size)
    base = (jnp.maximum(first, size) - size) * (me % 2)
    info = got_ref[pl.ds(group, 1), :]
    info = jnp.where(iota(info.shape, 1) == stride + 4, base, info)
    info_ref[...] = jnp.broadcast_to(info, info_ref.shape)
    asked = jnp.where(iota(heads.shape, 1) < stride, heads, rows_dev)
    high, low = (asked // 64).astype(f32).astype(bf16), (asked % 64).astype(f32).astype(bf16)
    chip_down, device_down = (u // 2).astype(f32), u.astype(f32)
    for number, wanted in enumerate((chip_down, peers - 1 - chip_down)):
        chosen = (rank == jnp.where(alone, device_down, wanted)).astype(f32)
        if number == 0:
            sent = jnp.sum(chosen * across, axis=1, keepdims=True)
            sent = jnp.where(alone, jnp.sum((across > 0.0).astype(f32)), sent)
            rows_ref[2] = jnp.broadcast_to(sent, (peers, wide)).astype(i32)
        chosen = chosen.astype(bf16)
        rows_ref[number] = (mul(chosen, high) * 64.0 + mul(chosen, low)).astype(i32)


def plan(got, sizes, stride, rows_dev):
    peers, length = got.shape
    wide = up_to_lanes(stride + 8)
    return pl.pallas_call(
        partial(plan_kernel, sizes, wide, stride, rows_dev),
        out_shape=(
            jax.ShapeDtypeStruct((1,), i32),
            jax.ShapeDtypeStruct((8, length), i32),
            jax.ShapeDtypeStruct((3, peers, wide), i32),
        ),
        in_specs=[in_vmem],
        out_specs=(in_smem, in_vmem, in_vmem),
        compiler_params=params(32),
        name="plan",
    )(got)


def block_rows(rows_ref, size, stride):
    first, second, first_size = rows_ref[0], rows_ref[1], rows_ref[2]
    lane, device = iota(first.shape, 1), iota(first.shape, 0)
    offset = jnp.maximum(first_size, size) - size
    after = second
    for shift in range(8, stride - size + 1, 8):
        after = jnp.where(offset == shift, pltpu.roll(second, shift, 1), after)
    if size < stride:
        rest = pltpu.roll(first, first.shape[1] - size, 1)
        after = jnp.where(lane < offset, rest, after)
    rows = jnp.where(device % 2 == 0, first, after)
    return jnp.where(lane < size, rows, -1)


def fetch_kernel(size, stride, rows_ref, table_ref, out_ref, packed):
    rows_dev = table_ref.shape[0]
    asked = block_rows(rows_ref, size, stride)
    for number in range(packed.shape[0]):
        packed[number] = asked[number * 8 : number * 8 + 8]
    row_of = iota((8 * size, rows_dev), 1)

    def block(number, carry):
        columns = jnp.transpose(packed[number])
        column = jnp.concatenate([columns[:size, j : j + 1] for j in range(8)], axis=0)
        picker = (column == row_of).astype(f32).astype(bf16)
        place = pl.ds(pl.multiple_of(number * 8 * size, 8 * size), 8 * size)
        out_ref[place, :] = mul(picker, table_ref[...]).astype(bf16)
        return carry

    blocks = packed.shape[0]
    if size == stride:
        blocks = pl.cdiv(active_devices(rows_ref), 8)

        def empty(number, carry):
            place = pl.ds(pl.multiple_of(number * 8 * size, 8 * size), 8 * size)
            out_ref[place, :] = jnp.zeros((8 * size, out_ref.shape[1]), bf16)
            return carry

        lax.fori_loop(blocks, packed.shape[0], empty, 0)
    lax.fori_loop(0, blocks, block, 0)


def active_devices(rows_ref):
    return jnp.max(rows_ref[2, 0:1, 0:1].astype(f32)).astype(i32)


def fetch(rows, table, size, stride):
    peers, wide = rows.shape[1:]
    return pl.pallas_call(
        partial(fetch_kernel, size, stride),
        out_shape=jax.ShapeDtypeStruct((peers * size, table.shape[1]), bf16),
        in_specs=[in_vmem, in_vmem],
        out_specs=in_vmem,
        scratch_shapes=[pltpu.VMEM((peers // 8, 8, wide), i32)],
        compiler_params=params(40),
        name="fetch",
    )(rows, table)


def train_kernel(
    wide, info_ref, come_ref, go_ref, stage, wide_ref, place_ref, left_ref, right_ref, live_ref,
    gl_ref, pg_ref, ps_ref, pr_ref
):
    peers, stride, features = come_ref.shape
    cap = stride // 3
    slots = peers * cap
    count = left_ref.shape[0]
    part = min(256, count)
    starts = range(0, count, part)

    def told(number):
        return info_ref[0:1, stride + number : stride + number + 1]

    base = jnp.sum(told(4).astype(f32)).astype(i32)
    bases = [base]
    for number in (2, 3):
        bases.append(base + jnp.sum(told(number).astype(f32)).astype(i32))
    bases = [pl.multiple_of(value, 8) for value in bases]
    for peer in range(peers):
        stage[peer, :stride, :] = come_ref[peer].astype(f32)
        stage[peer, stride:, :] = jnp.zeros((stage.shape[1] - stride, features), f32)
    for peer in range(peers):
        for kind in range(3):
            wide_ref[kind, peer * cap : peer * cap + cap, :] = stage[
                peer, pl.ds(bases[kind], cap), :
            ]
    packed_spots = info_ref[:, info_ref.shape[1] - count :]
    spot_rows = [(packed_spots // 4096).astype(f32), (packed_spots % 4096).astype(f32)]
    spot_columns = [jnp.transpose(rows) for rows in spot_rows]
    shared_down = jnp.transpose(info_ref[:, wide : wide + lanes].astype(f32))[:peers, 0:1]
    place = (iota((peers, slots), 1) - iota((peers, slots), 0) * cap).astype(f32)
    filled = ((place >= 0.0) & (place < shared_down)).astype(f32)
    fill = jnp.sum(filled, axis=0, keepdims=True)
    limit = told(1).astype(f32)
    live_across = (iota((1, count), 1).astype(f32) < limit).astype(f32)
    live_down = (iota((count, 1), 0).astype(f32) < limit).astype(f32)
    slot_across = iota((part, slots), 1).astype(f32)
    for kind, target in ((0, left_ref), (1, right_ref)):
        held = wide_ref[kind].astype(bf16)
        for start in starts:
            column = spot_columns[kind][start : start + part, 0:1]
            picker = (column == slot_across).astype(f32).astype(bf16)
            rows = mul(picker, held)
            target[start : start + part, :] = rows.astype(bf16)
            if kind == 1:
                rows = rows * live_down[start : start + part]
                live_ref[start : start + part, :] = rows.astype(bf16)
    shared_rows = wide_ref[2].astype(bf16)
    off_diagonal = (iota((part, part), 0) != iota((part, part), 1)).astype(f32)
    for start in starts:
        here = slice(start, start + part)
        left = left_ref[here, :]
        left_wide = left.astype(f32)
        right_wide = right_ref[here, :].astype(f32)
        pos_exp = jnp.exp(jnp.sum(left_wide * right_wide, axis=1, keepdims=True))
        shared_exp = jnp.exp(mul_t(left, shared_rows)) * fill
        total = pos_exp + jnp.sum(shared_exp, axis=1, keepdims=True)
        chunk_exps = []
        for other in starts:
            chunk_exp = jnp.exp(mul_t(left, right_ref[other : other + part, :]))
            if other == start:
                chunk_exp = chunk_exp * off_diagonal
            counted = chunk_exp * live_across[:, other : other + part]
            total = total + jnp.sum(counted, axis=1, keepdims=True)
            chunk_exps.append(chunk_exp)
        live = live_down[here]
        weight = live / total
        pos_grad = live * (pos_exp / total - 1.0)
        ps_ref[here, :] = (shared_exp * weight).astype(bf16)
        for other, chunk_exp in zip(starts, chunk_exps):
            pr_ref[here, other : other + part] = (chunk_exp * weight).astype(bf16)
        pull = mul(ps_ref[here, :], shared_rows) + mul(pr_ref[here, :], live_ref[...])
        gl_ref[here, :] = (pos_grad * right_wide + pull).astype(bf16)
        pg_ref[here, :] = pos_grad * left_wide
    left_turned = jnp.transpose(left_ref[...].astype(f32)).astype(bf16)
    place_ref[2] = jnp.transpose(mul(left_turned, ps_ref[...]))
    grad_right = jnp.transpose(mul(left_turned, pr_ref[...])) * live_down + pg_ref[...]
    right_ref[...] = grad_right.astype(bf16)
    slot_down = iota((part, count), 0).astype(f32)
    for kind, source in ((0, gl_ref), (1, right_ref)):
        for start in range(0, slots, part):
            picker = spot_rows[kind][0:1, :] - float(start) == slot_down
            picker = picker.astype(f32).astype(bf16)
            place_ref[kind, start : start + part, :] = mul(picker, source[...])
    stage[...] = jnp.zeros(stage.shape, f32)
    for kind in range(3):
        for peer in range(peers):
            stage[peer, pl.ds(bases[kind], cap), :] = place_ref[
                kind, peer * cap : peer * cap + cap, :
            ]
    for peer in range(peers):
        go_ref[peer] = stage[peer, :stride, :].astype(bf16)


def train(info, arrived, count, wide):
    peers, stride, features = arrived.shape
    cap = stride // 3
    slots = peers * cap
    return pl.pallas_call(
        partial(train_kernel, wide),
        out_shape=jax.ShapeDtypeStruct(arrived.shape, bf16),
        in_specs=[in_vmem, in_vmem],
        out_specs=in_vmem,
        scratch_shapes=[
            pltpu.VMEM((peers, stride + cap, features), f32),
            pltpu.VMEM((3, slots, features), f32),
            pltpu.VMEM((3, slots, features), f32),
            pltpu.VMEM((count, features), bf16),
            pltpu.VMEM((count, features), bf16),
            pltpu.VMEM((count, features), bf16),
            pltpu.VMEM((count, features), bf16),
            pltpu.VMEM((count, features), f32),
            pltpu.VMEM((count, slots), bf16),
            pltpu.VMEM((count, count), bf16),
        ],
        compiler_params=params(48),
        name="train",
    )(info, arrived)


def update_kernel(
    size, stride, rows_ref, back_ref, table_ref, state_ref, out_hbm, new_state_ref,
    turned, turned_new, grads_ref, out_ref, left
):
    peers, wide = rows_ref.shape[1:]
    rows_dev, features = table_ref.shape
    part = min(512, rows_dev)
    parts = rows_dev // part
    per_part = part // lanes
    asked = block_rows(rows_ref, size, stride) + 64
    length = peers * size
    spread = (iota((wide, length), 0) == iota((wide, length), 1) % size).astype(f32).astype(bf16)
    in_block = iota((peers, length), 1) // size == iota((peers, length), 0)
    flat = [
        jnp.sum(
            jnp.where(in_block, mul(digit.astype(f32).astype(bf16), spread), 0.0),
            axis=0,
            keepdims=True,
        )
        for digit in (asked // 64, asked % 64)
    ]
    flat = (flat[0] * 64.0 + flat[1]).astype(i32) - 64
    state_turned = jnp.transpose(state_ref[...])
    for number in range(parts):
        turned[number, :, :per_part] = state_turned[:, number * per_part : (number + 1) * per_part]

    def leave(number):
        rows = pl.ds(pl.multiple_of(number * part, part), part)
        return pltpu.make_async_copy(out_ref.at[rows], out_hbm.at[rows], left.at[number])

    def finish(number):
        grads = [grads_ref[j * lanes : (j + 1) * lanes, :] for j in range(per_part)]
        sums = [jnp.sum(g * g, axis=1, keepdims=True) for g in grads]
        state = turned[number, :, :per_part] + jnp.concatenate(sums, axis=1) * (1.0 / features)
        turned_new[number, :, :per_part] = state
        scale = learn_rate / (jnp.sqrt(state) + adagrad_eps)
        for j in range(per_part):
            place = pl.ds(pl.multiple_of(number * part + j * lanes, lanes), lanes)
            out_ref[place, :] = table_ref[place, :] - grads[j] * scale[:, j : j + 1]

    def with_length(length):
        def gather(number):
            picker = flat[:, :length] == iota((part, length), 0) + number * part
            return mul(picker.astype(f32).astype(bf16), back_ref[:length, :])

        def step(number, carry):
            finish(number - 1)
            grads_ref[...] = gather(number)
            leave(number - 1).start()
            return carry

        grads_ref[...] = gather(0)
        lax.fori_loop(1, parts, step, 0)

    if size == stride:
        most = peers * 3 // 4
        few = active_devices(rows_ref) <= most
        pl.when(few)(lambda: with_length(up_to_lanes(most * size)))
        pl.when(jnp.logical_not(few))(lambda: with_length(length))
    else:
        with_length(length)
    finish(parts - 1)
    leave(parts - 1).start()
    for number in range(parts):
        new_state_ref[number * per_part : (number + 1) * per_part, :] = jnp.transpose(
            turned_new[number]
        )[:per_part]
    for number in range(parts):
        leave(number).wait()


def update(rows, returned, table, state, size, stride):
    rows_dev, features = table.shape
    part = min(512, rows_dev)
    parts = rows_dev // part
    new_table, new_state = pl.pallas_call(
        partial(update_kernel, size, stride),
        out_shape=(
            jax.ShapeDtypeStruct(table.shape, f32),
            jax.ShapeDtypeStruct((rows_dev // lanes, lanes), f32),
        ),
        in_specs=[in_vmem, in_vmem, in_vmem, in_vmem],
        out_specs=(in_hbm, in_vmem),
        scratch_shapes=[
            pltpu.VMEM((parts, lanes, lanes), f32),
            pltpu.VMEM((parts, lanes, lanes), f32),
            pltpu.VMEM((part, features), f32),
            pltpu.VMEM(table.shape, f32),
            pltpu.SemaphoreType.DMA((parts,)),
        ],
        compiler_params=params(48),
        name="update",
    )(rows, returned, table, state.reshape(rows_dev // lanes, lanes))
    return new_table, new_state.reshape(rows_dev)


def body(
    embeddings,
    adagrad_state,
    edge_count,
    lhs_owner,
    lhs_row,
    rhs_owner,
    rhs_row,
    neg_owner,
    neg_row,
):
    axes = ("dom", "group")
    rows_dev, features = embeddings.shape
    group_len = lhs_row.shape[2]
    group_size = lax.axis_size("group")
    peers = lax.axis_size("dom") * group_size
    stride = 3 * (pl.cdiv(5 * group_len // (4 * peers), 8) * 8)
    half = pl.cdiv(stride // 2, 8) * 8
    sizes = sorted({half, min(half + 16, stride), min(half + 24, stride), stride})
    indices = [
        x.reshape(1, group_len)
        for x in (lhs_owner, lhs_row, rhs_owner, rhs_row, neg_owner, neg_row)
    ]

    def exchange(blocks):
        return lax.all_to_all(blocks, axes, split_axis=0, concat_axis=0, tiled=True)

    def bring(size):
        def run(rows, table16):
            answer = fetch(rows, table16, size, stride).reshape(peers, size, features)
            arrived = exchange(answer)
            if size == stride:
                return arrived
            to_first = [(core, core - 1) for core in range(1, group_size, 2)]
            extra = lax.ppermute(arrived[:, : stride - size], "group", to_first)
            return jnp.concatenate([arrived, extra], axis=1)

        return run

    def take(size):
        def run(rows, grads, table, state):
            over = stride - size
            outgoing = grads
            if over:
                to_second = [(core - 1, core) for core in range(1, group_size, 2)]
                passed = lax.ppermute(grads[:, size:], "group", to_second)
                outgoing = jnp.concatenate(
                    [grads[:, :over] + passed, grads[:, over:size]], axis=1
                )
            returned = exchange(outgoing).reshape(peers * size, features)
            return update(rows, returned, table, state, size, stride)

        return run

    got = exchange(prep(edge_count, indices, peers, stride, rows_dev)).reshape(peers, -1)
    choice, info, rows = plan(got, sizes, stride, rows_dev)
    number = choice[0]
    arrived = lax.switch(
        number, [bring(size) for size in sizes], rows, embeddings.astype(bf16)
    )
    grads = train(info, arrived, group_len, up_to_lanes(stride + 8))
    return lax.switch(
        number, [take(size) for size in sizes], rows, grads, embeddings, adagrad_state
    )


def solution(mesh):
    return jax.shard_map(
        body,
        mesh=mesh,
        in_specs=(
            P(("dom", "group"), None),
            P(("dom", "group")),
            P("dom"),
            P("dom", "group", None, None),
            P("dom", "group", None),
            P("dom", "group", None, None),
            P("dom", "group", None),
            P("dom", "group", None, None),
            P("dom", "group", None),
        ),
        out_specs=(P(("dom", "group"), None), P(("dom", "group"))),
        check_vma=False,
    )
```

time: 142 us -> 149 us (1.049)
  Pallas kernels: 29 us -> 32.9 us
  waiting for transfers between devices: 4.68 us -> 6.18 us
    pallas_call x4 -> x5, Pallas kernels: 29 us -> 32.9 us  [the longest x1 12.8 us: update(): pl.pallas_call(partial(update_kernel, size, stride), out_shape=(jax.Shape...]
    all_to_all x1, waiting for transfers between devices: 4.68 us -> 6.18 us  [exchange(): return lax.all_to_all(blocks, axes, split_axis=0, concat_axis=0, tiled=True)]
where the time goes in v4:
time: 149 us
  blocking collectives  97.3 us (65%)
  Pallas kernels  32.9 us (22%)
  starting transfers between devices  7.3 us (5%)
  waiting for transfers between devices  6.18 us (4%)
  other arithmetic  2.39 us (2%)
  between operations  2.16 us (1%)
    all_to_all x2, blocking collectives, exchange(): return lax.all_to_all(blocks, axes, split_axis=0, concat_axis=0, tiled=True)  97.3 us
    pallas_call x1, Pallas kernels, update(): pl.pallas_call(partial(update_kernel, size, stride), out_shape=(jax.Shape...  12.8 us
    pallas_call x1, Pallas kernels, train(): pl.pallas_call(partial(train_kernel, wide), out_shape=jax.ShapeDtypeStruc...  8.79 us
    pallas_call x1, Pallas kernels, fetch(): pl.pallas_call(partial(fetch_kernel, size, stride), out_shape=jax.ShapeDt...  7.62 us
    all_to_all x1, starting transfers between devices, exchange(): return lax.all_to_all(blocks, axes, split_axis=0, concat_axis=0, tiled=True)  7.3 us
    all_to_all x1, waiting for transfers between devices, exchange(): return lax.all_to_all(blocks, axes, split_axis=0, concat_axis=0, tiled=True)  6.18 us
  transfers between devices with their start and end apart: 1, of which 1 were waited for; matrix products, arithmetic and copies ran while one was open for 2% of the time, Pallas kernels for 0%

profile of v4, /device:TPU:0, one launch (start us, length us, event | category | flops | bytes accessed | tf_op | source)
XLA Modules:
  0.0 148.6 jit_solution(422774618604939553)
XLA Ops:
  1.3 2.9 %prep.1 = s32[32,1,1280]{2,1,0:T(1,128)} custom-call(s32[1]{0:T(128)S(6)} %copy.35.count_hbm, s32[1,1024]{1,0:T(1,128)} %bitcast.39, s32[1,1024]{1,0:T(1,128)} %bitcast.40, s32[1,1024]{1,0:T(1,128)} %bitcast.41, s32[1,1024]{1,0:T(1,128)} %bitcast.42, s32[1,1024]{1,0:T(1,128)} %bitcast.43, s32[1,1024]{1,0:T(1,128)} %bitcast.44), custom_call_target="tpu_custom_call" | custom-call | tf_op jit(solution)/shard_map/prep/pallas_call | solution.py:108
  4.2 7.3 %all-to-all-start.8 = ((s32[32,1,1280]{2,1,0:T(1,128)}), s32[32,1,1280]{2,1,0:T(1,128)S(1)}, u32[]{:S(2)}, u32[]{:S(2)}) async-start(s32[32,1,1280]{2,1,0:T(1,128)} %prep.1), calls=%async_computation.8 | async-start | bytes 327680 | tf_op jit(solution)/shard_map/all_to_all | solution.py:482
  11.5 2.4 %convert_element_type.3 = bf16[4096,256]{1,0:T(8,128)(2,1)S(1)} convert(f32[4096,256]{1,0:T(8,128)} %param.17) | non-fusion elementwise | flops 1048576 | bytes 6291456 | tf_op jit(solution)/shard_map/convert_element_type | solution.py:515
  13.9 6.2 %all-to-all-done.8 = s32[32,1,1280]{2,1,0:T(1,128)S(1)} async-done(((s32[32,1,1280]{2,1,0:T(1,128)}), s32[32,1,1280]{2,1,0:T(1,128)S(1)}, u32[]{:S(2)}, u32[]{:S(2)}) %all-to-all-start.8) | async-done | bytes 163872 | tf_op jit(solution)/shard_map/all_to_all | solution.py:482
  20.1 0.8 plan.1
  21.6 55.7 %conditional.2 = (bf16[32,120,256]{2,1,0:T(8,128)(2,1)S(1)}) conditional(s32[]{:T(128)} %bitcast.22, (s32[3,32,128]{2,1,0:T(8,128)S(1)}, bf16[4096,256]{1,0:T(8,128)(2,1)S(1)}) %tuple.35, (s32[3,32,128]{2,1,0:T(8,128)S(1)}, bf16[4096,256]{1,0:T(8,128)(2,1)S(1)}) %tuple.35, (s32[3,32,128]{2,1,0:T(8,128)S(1)}, ...), branch_computations={%region_0.0_spmd, %region_1.0_spmd, %region_2.0_spmd, %region_3.0_... | conditional | flops 3932160 | bytes 11534384 | solution.py:514
  21.6 7.6 %fetch.7 = bf16[3840,256]{1,0:T(8,128)(2,1)S(1)} custom-call(s32[3,32,128]{2,1,0:T(8,128)S(1)} %get-tuple-element.59.rows_ref, bf16[4096,256]{1,0:T(8,128)(2,1)S(1)} %get-tuple-element.60.table_ref), custom_call_target="tpu_custom_call" | custom-call | tf_op jit(solution)/shard_map/cond/branch_3_fun/fetch/pallas_call | solution.py:229
  29.2 48.0 %all_to_all.40 = bf16[32,120,256]{2,1,0:T(8,128)(2,1)S(1)} all-to-all(bf16[32,120,256]{2,1,0:T(8,128)(2,1)S(1)} %bitcast.27), channel_id=1, replica_groups=mesh['dom'=8,'group'=4] {'dom','group'}, dimensions={0} | all-to-all | bytes 3932160 | tf_op jit(solution)/shard_map/cond/branch_3_fun/all_to_all | solution.py:482
  77.2 0.0 copy-start.3
  77.2 8.8 %train.1 = bf16[32,120,256]{2,1,0:T(8,128)(2,1)S(1)} custom-call(s32[8,1280]{1,0:T(8,128)S(1)} %get-tuple-element.91.info_ref, bf16[32,120,256]{2,1,0:T(8,128)(2,1)S(1)} %get-tuple-element.112.come_ref), custom_call_target="tpu_custom_call" | custom-call | tf_op jit(solution)/shard_map/train/pallas_call | solution.py:339
  86.0 0.0 copy-done.3
  86.1 62.4 %conditional.3 = (f32[4096,256]{1,0:T(8,128)}, f32[4096]{0:T(1024)}) conditional(s32[]{:T(128)} %bitcast.22, (bf16[32,120,256]{2,1,0:T(8,128)(2,1)S(1)}, f32[4096]{0:T(1024)S(1)}, s32[3,32,128]{2,1,0:T(8,128)S(1)}, f32[4096,256]{1,0:T(8,128)}) %tuple.50, (bf16[32,120,256]{2,1,0:T(8,128)(2,1)S(1)}, ...), branch_computations={%region_4.0_spmd, %region_5.0_spmd, %region_6.0_spmd, %region_7.0_... | conditional | flops 3145728 | bytes 29491284 | solution.py:518
  86.3 49.3 %all_to_all.44 = bf16[32,120,256]{2,1,0:T(8,128)(2,1)S(1)} all-to-all(bf16[32,120,256]{2,1,0:T(8,128)(2,1)S(1)} %get-tuple-element.80), channel_id=1, replica_groups=mesh['dom'=8,'group'=4] {'dom','group'}, dimensions={0} | all-to-all | bytes 3932160 | tf_op jit(solution)/shard_map/cond/branch_3_fun/all_to_all | solution.py:482
  135.6 12.8 %update.7 = (f32[4096,256]{1,0:T(8,128)}, f32[32,128]{1,0:T(8,128)}) custom-call(s32[3,32,128]{2,1,0:T(8,128)S(1)} %get-tuple-element.79.rows_ref, bf16[3840,256]{1,0:T(8,128)(2,1)S(1)} %bitcast.26, f32[4096,256]{1,0:T(8,128)} %get-tuple-element.81.table_ref, f32[32,128]{1,0:T(8,128)S(1)} %bitcast.38), custom_call_target="tpu_custom_call" | custom-call | tf_op jit(solution)/shard_map/cond/branch_3_fun/update/pallas_call | solution.py:436
  (1 shorter events, 0.0 us)
Async XLA Ops:
  4.2 15.9 %all-to-all-start.8 = ((s32[32,1,1280]{2,1,0:T(1,128)}), s32[32,1,1280]{2,1,0:T(1,128)S(1)}, u32[]{:S(2)}, u32[]{:S(2)}) async-start(s32[32,1,1280]{2,1,0:T(1,128)} %prep.1), calls=%async_computation.8 | async-start | bytes 327680 | tf_op jit(solution)/shard_map/all_to_all | solution.py:482
  77.2 8.8 %copy-start.3 = (f32[4096]{0:T(1024)S(1)}, f32[4096]{0:T(1024)}, u32[]{:S(2)}) copy-start(f32[4096]{0:T(1024)} %param.18) | copy-start | bytes 49156

commit v5 on v4

--- a/solution.py
+++ b/solution.py
@@ -322,7 +322,7 @@
             picker = spot_rows[kind][0:1, :] - float(start) == slot_down
             picker = picker.astype(f32).astype(bf16)
             place_ref[kind, start : start + part, :] = mul(picker, source[...])
-    stage[...] = jnp.zeros(stage.shape, f32)
+    stage[:, :stride, :] = jnp.zeros((peers, stride, features), f32)
     for kind in range(3):
         for peer in range(peers):
             stage[peer, pl.ds(bases[kind], cap), :] = place_ref[
@@ -360,13 +360,22 @@
 
 def update_kernel(
     size, stride, rows_ref, back_ref, table_ref, state_ref, out_hbm, new_state_ref,
-    turned, turned_new, grads_ref, out_ref, left
+    turned, turned_new, grads_ref, out_ref, came, left
 ):
     peers, wide = rows_ref.shape[1:]
     rows_dev, features = table_ref.shape
+    staged = size == stride
     part = min(512, rows_dev)
     parts = rows_dev // part
     per_part = part // lanes
+
+    def come(number):
+        rows = pl.ds(pl.multiple_of(number * part, part), part)
+        return pltpu.make_async_copy(table_ref.at[rows], out_ref.at[rows], came.at[number])
+
+    if staged:
+        for number in range(parts):
+            come(number).start()
     asked = block_rows(rows_ref, size, stride) + 64
     length = peers * size
     spread = (iota((wide, length), 0) == iota((wide, length), 1) % size).astype(f32).astype(bf16)
@@ -389,6 +398,9 @@
         return pltpu.make_async_copy(out_ref.at[rows], out_hbm.at[rows], left.at[number])
 
     def finish(number):
+        if staged:
+            come(number).wait()
+        old_ref = out_ref if staged else table_ref
         grads = [grads_ref[j * lanes : (j + 1) * lanes, :] for j in range(per_part)]
         sums = [jnp.sum(g * g, axis=1, keepdims=True) for g in grads]
         state = turned[number, :, :per_part] + jnp.concatenate(sums, axis=1) * (1.0 / features)
@@ -396,7 +408,7 @@
         scale = learn_rate / (jnp.sqrt(state) + adagrad_eps)
         for j in range(per_part):
             place = pl.ds(pl.multiple_of(number * part + j * lanes, lanes), lanes)
-            out_ref[place, :] = table_ref[place, :] - grads[j] * scale[:, j : j + 1]
+            out_ref[place, :] = old_ref[place, :] - grads[j] * scale[:, j : j + 1]
 
     def with_length(length):
         def gather(number):
@@ -439,13 +451,14 @@
             jax.ShapeDtypeStruct(table.shape, f32),
             jax.ShapeDtypeStruct((rows_dev // lanes, lanes), f32),
         ),
-        in_specs=[in_vmem, in_vmem, in_vmem, in_vmem],
+        in_specs=[in_vmem, in_vmem, in_hbm if size == stride else in_vmem, in_vmem],
         out_specs=(in_hbm, in_vmem),
         scratch_shapes=[
             pltpu.VMEM((parts, lanes, lanes), f32),
             pltpu.VMEM((parts, lanes, lanes), f32),
             pltpu.VMEM((part, features), f32),
             pltpu.VMEM(table.shape, f32),
+            pltpu.SemaphoreType.DMA((parts,)),
             pltpu.SemaphoreType.DMA((parts,)),
         ],
         compiler_params=params(48),

time: 149 us -> 147 us (0.987)
  Pallas kernels: 32.9 us -> 30.5 us
    pallas_call x1, Pallas kernels: 12.8 us -> 10.5 us  [update(): pl.pallas_call(partial(update_kernel, size, stride), out_shape=(jax.Shape...]
where the time goes in v5:
time: 147 us; the launch traced here: 146 us
  blocking collectives  97.3 us (66%)
  Pallas kernels  30.5 us (21%)
  starting transfers between devices  7.3 us (5%)
  waiting for transfers between devices  6.18 us (4%)
  other arithmetic  2.39 us (2%)
  between operations  2.16 us (1%)
    all_to_all x2, blocking collectives, exchange(): return lax.all_to_all(blocks, axes, split_axis=0, concat_axis=0, tiled=True)  97.3 us
    pallas_call x1, Pallas kernels, update(): pl.pallas_call(partial(update_kernel, size, stride), out_shape=(jax.Shape...  10.5 us
    pallas_call x1, Pallas kernels, train(): pl.pallas_call(partial(train_kernel, wide), out_shape=jax.ShapeDtypeStruc...  8.7 us
    pallas_call x1, Pallas kernels, fetch(): pl.pallas_call(partial(fetch_kernel, size, stride), out_shape=jax.ShapeDt...  7.62 us
    all_to_all x1, starting transfers between devices, exchange(): return lax.all_to_all(blocks, axes, split_axis=0, concat_axis=0, tiled=True)  7.3 us
    all_to_all x1, waiting for transfers between devices, exchange(): return lax.all_to_all(blocks, axes, split_axis=0, concat_axis=0, tiled=True)  6.18 us
  transfers between devices with their start and end apart: 1, of which 1 were waited for; matrix products, arithmetic and copies ran while one was open for 2% of the time, Pallas kernels for 0%

profile of v5, /device:TPU:0, one launch (start us, length us, event | category | flops | bytes accessed | tf_op | source)
XLA Modules:
  0.0 146.2 jit_solution(8914211586057131511)
XLA Ops:
  1.3 2.9 %prep.1 = s32[32,1,1280]{2,1,0:T(1,128)} custom-call(s32[1]{0:T(128)S(6)} %copy.35.count_hbm, s32[1,1024]{1,0:T(1,128)} %bitcast.39, s32[1,1024]{1,0:T(1,128)} %bitcast.40, s32[1,1024]{1,0:T(1,128)} %bitcast.41, s32[1,1024]{1,0:T(1,128)} %bitcast.42, s32[1,1024]{1,0:T(1,128)} %bitcast.43, s32[1,1024]{1,0:T(1,128)} %bitcast.44), custom_call_target="tpu_custom_call" | custom-call | tf_op jit(solution)/shard_map/prep/pallas_call | solution.py:108
  4.2 7.3 %all-to-all-start.8 = ((s32[32,1,1280]{2,1,0:T(1,128)}), s32[32,1,1280]{2,1,0:T(1,128)S(1)}, u32[]{:S(2)}, u32[]{:S(2)}) async-start(s32[32,1,1280]{2,1,0:T(1,128)} %prep.1), calls=%async_computation.8 | async-start | bytes 327680 | tf_op jit(solution)/shard_map/all_to_all | solution.py:495
  11.5 2.4 %convert_element_type.3 = bf16[4096,256]{1,0:T(8,128)(2,1)S(1)} convert(f32[4096,256]{1,0:T(8,128)} %param.17) | non-fusion elementwise | flops 1048576 | bytes 6291456 | tf_op jit(solution)/shard_map/convert_element_type | solution.py:528
  13.9 6.2 %all-to-all-done.8 = s32[32,1,1280]{2,1,0:T(1,128)S(1)} async-done(((s32[32,1,1280]{2,1,0:T(1,128)}), s32[32,1,1280]{2,1,0:T(1,128)S(1)}, u32[]{:S(2)}, u32[]{:S(2)}) %all-to-all-start.8) | async-done | bytes 163872 | tf_op jit(solution)/shard_map/all_to_all | solution.py:495
  20.1 0.8 plan.1
  21.6 55.7 %conditional.2 = (bf16[32,120,256]{2,1,0:T(8,128)(2,1)S(1)}) conditional(s32[]{:T(128)} %bitcast.22, (s32[3,32,128]{2,1,0:T(8,128)S(1)}, bf16[4096,256]{1,0:T(8,128)(2,1)S(1)}) %tuple.35, (s32[3,32,128]{2,1,0:T(8,128)S(1)}, bf16[4096,256]{1,0:T(8,128)(2,1)S(1)}) %tuple.35, (s32[3,32,128]{2,1,0:T(8,128)S(1)}, ...), branch_computations={%region_0.0_spmd, %region_1.0_spmd, %region_2.0_spmd, %region_3.0_... | conditional | flops 3932160 | bytes 11534384 | solution.py:527
  21.6 7.6 %fetch.7 = bf16[3840,256]{1,0:T(8,128)(2,1)S(1)} custom-call(s32[3,32,128]{2,1,0:T(8,128)S(1)} %get-tuple-element.59.rows_ref, bf16[4096,256]{1,0:T(8,128)(2,1)S(1)} %get-tuple-element.60.table_ref), custom_call_target="tpu_custom_call" | custom-call | tf_op jit(solution)/shard_map/cond/branch_3_fun/fetch/pallas_call | solution.py:229
  29.2 48.0 %all_to_all.40 = bf16[32,120,256]{2,1,0:T(8,128)(2,1)S(1)} all-to-all(bf16[32,120,256]{2,1,0:T(8,128)(2,1)S(1)} %bitcast.27), channel_id=1, replica_groups=mesh['dom'=8,'group'=4] {'dom','group'}, dimensions={0} | all-to-all | bytes 3932160 | tf_op jit(solution)/shard_map/cond/branch_3_fun/all_to_all | solution.py:495
  77.2 0.0 copy-start.3
  77.2 8.7 %train.1 = bf16[32,120,256]{2,1,0:T(8,128)(2,1)S(1)} custom-call(s32[8,1280]{1,0:T(8,128)S(1)} %get-tuple-element.91.info_ref, bf16[32,120,256]{2,1,0:T(8,128)(2,1)S(1)} %get-tuple-element.112.come_ref), custom_call_target="tpu_custom_call" | custom-call | tf_op jit(solution)/shard_map/train/pallas_call | solution.py:339
  86.0 0.0 copy-done.3
  86.0 60.1 %conditional.3 = (f32[4096,256]{1,0:T(8,128)}, f32[4096]{0:T(1024)}) conditional(s32[]{:T(128)} %bitcast.22, (bf16[32,120,256]{2,1,0:T(8,128)(2,1)S(1)}, f32[4096]{0:T(1024)S(1)}, s32[3,32,128]{2,1,0:T(8,128)S(1)}, f32[4096,256]{1,0:T(8,128)}) %tuple.50, (bf16[32,120,256]{2,1,0:T(8,128)(2,1)S(1)}, ...), branch_computations={%region_4.0_spmd, %region_5.0_spmd, %region_6.0_spmd, %region_7.0_... | conditional | flops 3145728 | bytes 29491284 | solution.py:531
  86.2 49.3 %all_to_all.44 = bf16[32,120,256]{2,1,0:T(8,128)(2,1)S(1)} all-to-all(bf16[32,120,256]{2,1,0:T(8,128)(2,1)S(1)} %get-tuple-element.80), channel_id=1, replica_groups=mesh['dom'=8,'group'=4] {'dom','group'}, dimensions={0} | all-to-all | bytes 3932160 | tf_op jit(solution)/shard_map/cond/branch_3_fun/all_to_all | solution.py:495
  135.5 10.5 %update.7 = (f32[4096,256]{1,0:T(8,128)}, f32[32,128]{1,0:T(8,128)}) custom-call(s32[3,32,128]{2,1,0:T(8,128)S(1)} %get-tuple-element.79.rows_ref, bf16[3840,256]{1,0:T(8,128)(2,1)S(1)} %bitcast.26, f32[4096,256]{1,0:T(8,128)} %get-tuple-element.81.table_ref, f32[32,128]{1,0:T(8,128)S(1)} %bitcast.38), custom_call_target="tpu_custom_call" | custom-call | tf_op jit(solution)/shard_map/cond/branch_3_fun/update/pallas_call | solution.py:448
  (1 shorter events, 0.0 us)
Async XLA Ops:
  4.2 15.9 %all-to-all-start.8 = ((s32[32,1,1280]{2,1,0:T(1,128)}), s32[32,1,1280]{2,1,0:T(1,128)S(1)}, u32[]{:S(2)}, u32[]{:S(2)}) async-start(s32[32,1,1280]{2,1,0:T(1,128)} %prep.1), calls=%async_computation.8 | async-start | bytes 327680 | tf_op jit(solution)/shard_map/all_to_all | solution.py:495
  77.2 8.7 %copy-start.3 = (f32[4096]{0:T(1024)S(1)}, f32[4096]{0:T(1024)}, u32[]{:S(2)}) copy-start(f32[4096]{0:T(1024)} %param.18) | copy-start | bytes 49156
